TPU v7x, 32 devices: a whole 2x2x4 slice. The times are simulated.
32 devices in a mesh: dp: 4 (over z), brick: 8 (over y, x, core).
Axes of the slice: x: 2, y: 2, z: 4, core: 2. Of those that a mesh axis runs over, the one named last changes fastest.
Arguments:
- records: bfloat16 [32, 8, 16, 6144], P(('dp', 'brick')), may hold values from -6 to 6
- positions: int32 [32, 8, 16], P(('dp', 'brick')), may hold values from -1 to 127, as said below
- weight: bfloat16 [2592, 192], P('dp'), may hold values from -0.125 to 0.125
- cotangent: bfloat16 [4, 32, 16, 3072], P('dp', 'brick'), may hold values from -0.0234375 to 0.0234375
Outputs:
- activation: bfloat16 [4, 32, 16, 3072], P('dp', 'brick')
- weight_grad: float32 [2592, 192], P('dp')
Inputs may be any that keep to these rules, and one draw needn't show every extreme that they name: Entry [d * 8 + s, o, r] is the brick position in owner o's slab of scene d of the r-th record that source s sends to o, or -1 for an empty slot. The live positions at one owner of one scene are distinct; in every scene some owner has all 128 of its slots filled.
All inputs are finite; a program needn't handle non-finite values.
Results may differ from a plain program's by a relative error of at most 0.0029.
Values may be sent and summed in bfloat16 or wider, within the bound.
A program may use at most 64 MiB of HBM per device.

v0:
```python
import jax
import jax.numpy as jnp
from jax import lax
from jax.sharding import PartitionSpec as P

C_IN = 96
BS = 4
BX = 2
BY = 8
BZ = 8


def from_behind(block, axis, distance):
    devices = range(lax.axis_size(axis))
    route = [(i - distance, i) for i in devices if i - distance in devices]
    return lax.ppermute(block, axis, route)


def place_records(arrived, places, brick_x, brick_y, brick_z, side, channels):
    count = brick_x * brick_y * brick_z
    target = jnp.where(places >= 0, places, count)
    filled = jnp.zeros((count + 1, arrived.shape[1]), arrived.dtype).at[target].set(arrived)[:count]
    cubes = filled.reshape(brick_x, brick_y, brick_z, side, side, side, channels)
    cubes = cubes.transpose(0, 3, 1, 4, 2, 5, 6)
    return cubes.reshape(brick_x * side, brick_y * side, brick_z * side, channels)


def parity_split(voxels, boundary):
    padded = jnp.concatenate([boundary, voxels], axis=0)
    padded = jnp.pad(padded, ((0, 1), (1, 1), (1, 1), (0, 0)))
    half_x = padded.shape[0] // 2
    half_y = padded.shape[1] // 2
    half_z = padded.shape[2] // 2
    channels = padded.shape[3]
    split = padded.reshape(half_x, 2, half_y, 2, half_z, 2, channels)
    return split.transpose(1, 3, 5, 0, 2, 4, 6)


def column_block(classes, out_x, out_y, out_z):
    channels = classes.shape[-1]
    taps = []
    for offset_x in range(3):
        for offset_y in range(3):
            for offset_z in range(3):
                picked = classes[
                    offset_x % 2,
                    offset_y % 2,
                    offset_z % 2,
                    offset_x // 2 : offset_x // 2 + out_x,
                    offset_y // 2 : offset_y // 2 + out_y,
                    offset_z // 2 : offset_z // 2 + out_z,
                ]
                taps.append(picked.reshape(out_x * out_y * out_z, channels))
    return jnp.concatenate(taps, axis=1)


def body(records, positions, weight, cotangent):
    arrived, places = (
        lax.all_to_all(records, "brick", split_axis=1, concat_axis=0, tiled=True),
        lax.all_to_all(
            positions.astype(jnp.bfloat16), "brick", split_axis=1, concat_axis=0, tiled=True
        ),
    )
    arrived = arrived.reshape(-1, arrived.shape[-1])
    places = places.reshape(-1).astype(jnp.int32)
    voxels = place_records(arrived, places, BX, BY, BZ, BS, C_IN)
    boundary = from_behind(voxels[voxels.shape[0] - 1 :], "brick", 1)
    out_x = voxels.shape[0] // 2
    out_y = voxels.shape[1] // 2
    out_z = voxels.shape[2] // 2
    columns = column_block(parity_split(voxels, boundary), out_x, out_y, out_z)
    full_weight = lax.all_gather(weight, "dp", axis=0, tiled=True)
    linear = jnp.dot(columns, full_weight, preferred_element_type=jnp.float32)
    activation = jax.nn.silu(linear).astype(jnp.bfloat16)
    sigma = jax.nn.sigmoid(linear)
    slope = sigma * (1.0 + linear * (1.0 - sigma))
    upstream = cotangent.reshape(linear.shape[0], weight.shape[1])
    slope_grad = (upstream.astype(jnp.float32) * slope).astype(jnp.bfloat16)
    partial_grad = lax.dot_general(
        columns, slope_grad, (((0,), (0,)), ((), ())), preferred_element_type=jnp.float32
    )
    summed = lax.psum(partial_grad, "brick")
    weight_grad = lax.psum_scatter(summed, "dp", scatter_dimension=0, tiled=True)
    return (activation.reshape(cotangent.shape), weight_grad)


def solution(mesh):
    placed = (
        P(("dp", "brick"), None, None, None),
        P(("dp", "brick"), None, None),
        P("dp", None),
        P("dp", "brick", None, None),
    )
    return jax.shard_map(
        body,
        mesh=mesh,
        in_specs=placed,
        out_specs=(P("dp", "brick", None, None), P("dp", None)),
        check_vma=False,
    )
```

profile of v0, /device:TPU:25, one launch (start us, length us, event | category | flops | bytes accessed | tf_op | source)
XLA Modules:
  0.0 232.2 jit_solution(11437274656775000039)
XLA Ops:
  7.9 8.1 %all_to_all.8 = bf16[1,8,16]{2,0,1:T(2,128)(2,1)S(1)} all-to-all(bf16[1,8,16]{2,0,1:T(2,128)(2,1)S(1)} %copy.22), channel_id=1, replica_groups=mesh['dp'=4,'brick'=8] {'brick'}, dimensions={1} | all-to-all | bytes 512 | tf_op jit(solution)/shard_map/all_to_all | solution.py:60
  16.0 4.2 %all-to-all-start.1 = ((bf16[1,8,16,6144]{3,2,0,1:T(8,128)(2,1)}), bf16[1,8,16,6144]{3,2,0,1:T(8,128)(2,1)S(1)}, u32[]{:S(2)}, u32[]{:S(2)}) async-start(bf16[1,8,16,6144]{3,2,0,1:T(8,128)(2,1)} %bitcast.50), calls=%async_computation.1 | async-start | bytes 3145728 | tf_op jit(solution)/shard_map/all_to_all | solution.py:59
  20.3 17.4 %all-to-all-done.1 = bf16[1,8,16,6144]{3,2,0,1:T(8,128)(2,1)S(1)} async-done(((bf16[1,8,16,6144]{3,2,0,1:T(8,128)(2,1)}), bf16[1,8,16,6144]{3,2,0,1:T(8,128)(2,1)S(1)}, u32[]{:S(2)}, u32[]{:S(2)}) %all-to-all-start.1) | async-done | bytes 1572896 | tf_op jit(solution)/shard_map/all_to_all | solution.py:59
  37.7 3.2 %scatter_custom_fusion = bf16[129,6144]{1,0:T(8,128)(2,1)S(1)} fusion(s32[128]{0:T(128)S(1)} %fusion.15, bf16[128,6144]{1,0:T(8,128)(2,1)S(1)} %bitcast.51, bf16[]{:T(256)} %constant.5.clone.1), kind=kCustom, calls=%fused_computation.18 | custom fusion | bytes 1585154 | tf_op jit(solution)/shard_map/scatter | solution.py:22
  40.9 1.3 slice.116
  42.1 4.4 %reshape.59 = bf16[2,8,8,4,4,4,96]{6,5,4,3,2,1,0:T(4,128)(2,1)S(1)} reshape(bf16[128,6144]{1,0:T(8,128)(2,1)} %slice.116) | data formatting | bytes 3145728 | tf_op jit(solution)/shard_map/reshape | solution.py:23
  47.7 1.3 copy-done
  49.1 5.6 %collective-permute-start = (bf16[1,32,32,96]{3,2,1,0:T(8,128)(2,1)S(1)}, bf16[1,32,32,96]{3,2,1,0:T(8,128)(2,1)}, u32[]{:S(2)}, u32[]{:S(2)}) collective-permute-start(bf16[1,32,32,96]{3,2,1,0:T(8,128)(2,1)S(1)} %slice.117), channel_id=1, source_target_pairs={{0,1},{1,2},{2,3},{3,4},{4,5},{5,6},{6,7},{8,9},{9,10},{10,11},{11... | collective-permute-start | bytes 589832 | tf_op jit(solution)/shard_map/ppermute | solution.py:16
  54.6 24.0 %all-gather = bf16[4,648,192]{1,2,0:T(8,128)(2,1)S(1)} all-gather(bf16[1,648,192]{1,2,0:T(8,128)(2,1)S(1)} %bitcast.79), channel_id=1, replica_groups=mesh['dp'=4,'brick'=8] {'dp'}, dimensions={0}, use_global_device_ids=true | all-gather | bytes 1244160 | tf_op jit(solution)/shard_map/all_gather | solution.py:72
  79.5 1.7 reshape.74
  81.7 1.2 copy.28
  83.0 3.4 %fusion.8 = bf16[10,34,34,96]{3,2,1,0:T(8,128)(2,1)S(1)} fusion(bf16[8,32,32,96]{3,2,1,0:T(8,128)(2,1)} %bitcast.48, bf16[1,32,32,96]{3,2,1,0:T(8,128)(2,1)} %collective-permute-done), kind=kLoop, calls=%fused_computation.15 | loop fusion | flops 21085440 | bytes 3988992 | tf_op jit(solution)/shard_map/concatenate | solution.py:29
  86.3 3.2 %reshape.61 = bf16[5,2,17,2,17,2,96]{6,5,4,3,2,1,0:T(2,128)(2,1)} reshape(bf16[10,34,34,96]{3,2,1,0:T(8,128)(2,1)S(1)} %fusion.8) | data formatting | bytes 4439040 | tf_op jit(solution)/shard_map/reshape | solution.py:35
  89.5 2.4 %copy.32 = bf16[5,2,17,2,17,2,96]{6,4,2,0,5,3,1:T(8,128)(2,1)S(1)} copy(bf16[5,2,17,2,17,2,96]{6,5,4,3,2,1,0:T(2,128)(2,1)} %reshape.61) | data formatting | bytes 4439040 | tf_op jit(solution)/shard_map/reshape | solution.py:35
  91.9 1.8 fusion.17
  93.7 1.4 fusion.18
  95.1 10.1 %concatenate.7 = bf16[1024,2592]{1,0:T(8,128)(2,1)} concatenate(bf16[1024,96]{1,0:T(8,128)(2,1)} %bitcast.78, bf16[1024,96]{1,0:T(8,128)(2,1)} %bitcast.77, bf16[1024,96]{1,0:T(8,128)(2,1)} %bitcast.76, bf16[1024,96]{1,0:T(8,128)(2,1)} %bitcast.75, bf16[1024,96]{1,0:T(8,128)(2,1)} %bitcast.74, bf16[1024,96]{1,0:T(8,128)(2,1)} %bitcast.73, bf16[1024,96]{1,0:T(8,128)(2,1)} %bitcast.72, ...), dimensions={1} | concatenate | bytes 10616832 | tf_op jit(solution)/shard_map/concatenate | solution.py:54
  105.2 5.0 %multiply_convert_fusion.1 = (bf16[1024,192]{0,1:T(8,128)(2,1)S(1)}, f32[1024,192]{0,1:T(8,128)S(1)}) fusion(bf16[1024,2592]{1,0:T(8,128)(2,1)} %concatenate.7, bf16[2592,192]{0,1:T(8,128)(2,1)} %reshape.74), kind=kOutput, calls=%fused_computation.21 | convolution fusion | flops 1020198912 | bytes 7483392 | tf_op jit(solution)/shard_map/dot_general | solution.py:73
  110.2 3.9 %fusion.13 = f32[2592,192]{1,0:T(8,128)} fusion(bf16[1024,2592]{1,0:T(8,128)(2,1)S(1)} %copy-done.1, f32[1024,192]{0,1:T(8,128)S(1)} %copy-done.2, f32[1024,192]{0,1:T(8,128)S(1)} %get-tuple-element.30), kind=kOutput, calls=%fused_computation.23 | convolution fusion | flops 1020985344 | bytes 8871936
  114.1 50.6 %reduce-scatter.4.cloned.1.call-done = f32[648,192]{1,0:T(8,128)} async-done(((f32[2592,192]{1,0:T(8,128)}), f32[648,192]{1,0:T(8,128)}) %reduce-scatter.4.cloned.1.call-update) | async-done | bytes 497680
  164.8 2.2 copy.30
  167.1 1.3 reshape.62
  168.4 55.0 %all-reduce.3.cloned.1.call-done = f32[648,192]{0,1:T(8,128)} async-done(((f32[648,192]{0,1:T(8,128)}), f32[648,192]{0,1:T(8,128)}) %all-reduce.3.cloned.1.call-update) | async-done | bytes 497680 | tf_op jit(solution)/shard_map/psum | solution.py:82
  223.4 1.9 copy.34
  (24 shorter events, 3.7 us)
Async XLA Ops:
  16.0 21.7 %all-to-all-start.1 = ((bf16[1,8,16,6144]{3,2,0,1:T(8,128)(2,1)}), bf16[1,8,16,6144]{3,2,0,1:T(8,128)(2,1)S(1)}, u32[]{:S(2)}, u32[]{:S(2)}) async-start(bf16[1,8,16,6144]{3,2,0,1:T(8,128)(2,1)} %bitcast.50), calls=%async_computation.1 | async-start | bytes 3145728 | tf_op jit(solution)/shard_map/all_to_all | solution.py:59
  20.2 144.6 %reduce-scatter.4.cloned.1.call-start = ((), (), s32[]{:S(2)}) async-start(), calls=%async_computation.4 | async-start | bytes 3317760
  42.1 12.5 %copy-start.4 = (bf16[648,192]{0,1:T(8,128)(2,1)S(1)}, bf16[648,192]{0,1:T(8,128)(2,1)}, u32[]{:S(2)}) copy-start(bf16[648,192]{0,1:T(8,128)(2,1)} %param.6) | copy-start | bytes 746500
  47.7 1.4 copy-start
  47.7 33.5 %copy-start.3 = (bf16[1,4,16,3072]{3,2,1,0:T(8,128)(2,1)S(1)}, bf16[1,4,16,3072]{3,2,1,0:T(8,128)(2,1)}, u32[]{:S(2)}) copy-start(bf16[1,4,16,3072]{3,2,1,0:T(8,128)(2,1)} %param.7) | copy-start | bytes 1179652
  49.1 33.9 %collective-permute-start = (bf16[1,32,32,96]{3,2,1,0:T(8,128)(2,1)S(1)}, bf16[1,32,32,96]{3,2,1,0:T(8,128)(2,1)}, u32[]{:S(2)}, u32[]{:S(2)}) collective-permute-start(bf16[1,32,32,96]{3,2,1,0:T(8,128)(2,1)S(1)} %slice.117), channel_id=1, source_target_pairs={{0,1},{1,2},{2,3},{3,4},{4,5},{5,6},{6,7},{8,9},{9,10},{10,11},{11... | collective-permute-start | bytes 589832 | tf_op jit(solution)/shard_map/ppermute | solution.py:16
  105.1 5.0 %copy-start.1 = (bf16[1024,2592]{1,0:T(8,128)(2,1)S(1)}, bf16[1024,2592]{1,0:T(8,128)(2,1)}, u32[]{:S(2)}) copy-start(bf16[1024,2592]{1,0:T(8,128)(2,1)} %concatenate.7) | copy-start | bytes 15925252
  105.1 5.0 %copy-start.2 = (f32[1024,192]{0,1:T(8,128)S(1)}, f32[1024,192]{0,1:T(8,128)}, u32[]{:S(2)}) copy-start(f32[1024,192]{0,1:T(8,128)} %copy.28) | copy-start | bytes 2359300
  114.1 109.3 %all-reduce.3.cloned.1.call-start = ((), (), s32[]{:S(2)}) async-start(), calls=%async_computation.3 | async-start | bytes 1179648 | tf_op jit(solution)/shard_map/psum | solution.py:82
Sparse Core Ops, SparseCore 0:
  114.2 50.4 reduce-scatter.3
  168.5 54.9 all-reduce.2
where the time goes:
time: 236 us; the launch traced here: 232 us
  waiting for transfers between devices  123 us (52%)
  local copies, waits for them, and re-layouts  40.1 us (17%)
  blocking collectives  32.1 us (14%)
  between operations  14.2 us (6%)
  starting transfers between devices  9.78 us (4%)
  matrix products  8.89 us (4%)
  other arithmetic  4.07 us (2%)
    psum x1, waiting for transfers between devices, body(): summed = lax.psum(partial_grad, 'brick')  55 us
    unnamed x3, waiting for transfers between devices  50.6 us
    all_gather x1, blocking collectives, body(): full_weight = lax.all_gather(weight, 'dp', axis=0, tiled=True)  24 us
    all_to_all x1, waiting for transfers between devices, body(): lax.all_to_all(records, 'brick', split_axis=1, concat_axis=0, tiled=True)  17.4 us
    concatenate x1, local copies, waits for them, and re-layouts, column_block(): return jnp.concatenate(taps, axis=1)  10.1 us
    all_to_all x1, blocking collectives, body(): lax.all_to_all(positions.astype(jnp.bfloat16), 'brick', split_axis=1, con...  8.14 us
    unnamed x13, local copies, waits for them, and re-layouts  7.13 us
    reshape x2, local copies, waits for them, and re-layouts, parity_split(): split = padded.reshape(half_x, 2, half_y, 2, half_z, 2, channels)  5.58 us
  transfers between devices with their start and end apart: 4, of which 3 were waited for; matrix products, arithmetic and copies ran while one was open for 3% of the time, Pallas kernels for 0%

commit v1 on v0

v1 whole, which is shorter than its diff:
```python
import functools

import jax
import jax.numpy as jnp
from jax import lax
from jax.experimental import pallas as pl
from jax.experimental.pallas import tpu as pltpu
from jax.sharding import PartitionSpec as P

C_IN = 96
C_OUT = 192
BS = 4
BX = 2
BY = 8
BZ = 8
TAPS = 27
PLANE = BS * BS * C_IN
ROW = BS * C_IN
KB = 512
NB = 256
MESH = pl.DeviceIdType.MESH
VMEM_LIMIT = 48 * 1024 * 1024


def up(n, k):
    return -(-n // k) * k


def copy_to(src, dst, send, recv, axis, peer):
    return pltpu.make_async_remote_copy(
        src_ref=src, dst_ref=dst, send_sem=send, recv_sem=recv,
        device_id={axis: peer}, device_id_type=MESH,
    )


def exchange_kernel(nb, nd, half, rec, pos, wt, rec_out, pos_out, wt_out,
                    rs, rr, ps, pr, ws, wr, xs, xr, loc):
    me = lax.axis_index("brick")
    dp = lax.axis_index("dp")
    core = lax.rem(me, 2)
    sib = me + 1 - 2 * core
    barrier = pltpu.get_barrier_semaphore()
    for k in range(1, nb):
        pl.semaphore_signal(barrier, inc=1, device_id={"brick": lax.rem(me + k, nb)}, device_id_type=MESH)
    for k in range(1, nd):
        pl.semaphore_signal(barrier, inc=1, device_id={"dp": lax.rem(dp + k, nd)}, device_id_type=MESH)
    own = [
        pltpu.make_async_copy(rec.at[me], rec_out.at[me], loc.at[0]),
        pltpu.make_async_copy(pos.at[me], pos_out.at[me], loc.at[1]),
        pltpu.make_async_copy(wt, wt_out.at[dp], loc.at[2]),
    ]
    for c in own:
        c.start()
    pl.semaphore_wait(barrier, nb + nd - 2)
    mine = pl.ds(pl.multiple_of(core * half, 16), half)
    sent = []
    for k in range(1, nd):
        o = lax.rem(dp + k, nd)
        c = copy_to(wt.at[mine], wt_out.at[dp, mine], ws.at[k], wr.at[k], "dp", o)
        c.start()
        sent.append(c)
    for k in range(1, nb):
        o = lax.rem(me + k, nb)
        c = copy_to(pos.at[o], pos_out.at[me], ps.at[k], pr.at[k], "brick", o)
        c.start()
        sent.append(c)
        c = copy_to(rec.at[o], rec_out.at[me], rs.at[k], rr.at[k], "brick", o)
        c.start()
        sent.append(c)
    theirs = pl.ds(pl.multiple_of((1 - core) * half, 16), half)
    for k in range(1, nd):
        s = lax.rem(dp + nd - k, nd)
        copy_to(wt.at[mine], wt_out.at[s, mine], ws.at[k], wr.at[k], "dp", s).wait_recv()
        c = copy_to(wt_out.at[s, mine], wt_out.at[s, mine], xs.at[k], xr.at[k], "brick", sib)
        c.start()
        sent.append(c)
    for k in range(1, nd):
        s = lax.rem(dp + nd - k, nd)
        copy_to(wt.at[theirs], wt_out.at[s, theirs], xs.at[k], xr.at[k], "brick", sib).wait_recv()
    for k in range(1, nb):
        s = lax.rem(me + nb - k, nb)
        copy_to(pos.at[s], pos_out.at[s], ps.at[k], pr.at[k], "brick", s).wait_recv()
        copy_to(rec.at[s], rec_out.at[s], rs.at[k], rr.at[k], "brick", s).wait_recv()
    for c in sent:
        c.wait_send()
    for c in own:
        c.wait()


def exchange(rec, pos, wt, nb, nd):
    half = wt.shape[0] // 2
    dma = pltpu.SemaphoreType.DMA
    return pl.pallas_call(
        functools.partial(exchange_kernel, nb, nd, half),
        out_shape=(
            jax.ShapeDtypeStruct(rec.shape, rec.dtype),
            jax.ShapeDtypeStruct(pos.shape, pos.dtype),
            jax.ShapeDtypeStruct((nd,) + wt.shape, wt.dtype),
        ),
        in_specs=[pl.BlockSpec(memory_space=pl.ANY)] * 3,
        out_specs=(pl.BlockSpec(memory_space=pl.ANY),) * 3,
        scratch_shapes=[dma((nb,)), dma((nb,)), dma((nb,)), dma((nb,)),
                        dma((nd,)), dma((nd,)), dma((nd,)), dma((nd,)), dma((3,))],
        compiler_params=pltpu.CompilerParams(collective_id=0, has_side_effects=True),
        name="exchange",
    )(rec, pos, wt)


def place_kernel(arrived, places, filled, rim):
    n = filled.shape[0]
    slots = arrived.shape[0]
    want = lax.broadcasted_iota(jnp.int32, (n, slots), 0)
    pick = jnp.where(places[...] == want, 1.0, 0.0).astype(jnp.bfloat16)
    for x in range(BS):
        lanes = slice(x * PLANE, (x + 1) * PLANE)
        part = jnp.dot(pick, arrived[:, lanes], preferred_element_type=jnp.float32).astype(jnp.bfloat16)
        filled[:, lanes] = part
        if x == BS - 1:
            rim[...] = part[n - n // BX:]


def place(arrived, places):
    n = BX * BY * BZ
    return pl.pallas_call(
        place_kernel,
        out_shape=(
            jax.ShapeDtypeStruct((n, arrived.shape[1]), arrived.dtype),
            jax.ShapeDtypeStruct((n // BX, PLANE), arrived.dtype),
        ),
        compiler_params=pltpu.CompilerParams(vmem_limit_bytes=VMEM_LIMIT),
        name="place",
    )(arrived, places)


def shift_matrix(n, dy, dz):
    r = lax.broadcasted_iota(jnp.int32, (n, n), 0)
    c = lax.broadcasted_iota(jnp.int32, (n, n), 1)
    hit = c == r - dy * BZ - dz
    if dy:
        hit = hit & (lax.rem(r // BZ, BY) > 0)
    if dz:
        hit = hit & (lax.rem(r, BZ) > 0)
    return jnp.where(hit, 1.0, 0.0).astype(jnp.bfloat16)


def row_parts(first, count, shard):
    done = 0
    while done < count:
        d, r = divmod(first + done, shard)
        take = min(count - done, shard - r)
        yield d, r, take, done
        done += take


def layer_kernel(nd, shard, cut, piece, filled, rim, wt, cot, act, terms, cols, band, slopes):
    n = filled.shape[0]
    rows = 4 * n
    f32, bf16 = jnp.float32, jnp.bfloat16
    band[...] = jnp.zeros_like(band)
    slopes[...] = jnp.zeros_like(slopes)
    terms[...] = jnp.zeros_like(terms)
    spots = {0: ((KB - C_IN, 0), (C_IN, NB)), 1: ((0, 0), (2 * C_IN, NB)), 2: ((C_IN, 0), (3 * C_IN, NB))}
    for t in range(TAPS):
        ab, e = divmod(t, 3)
        for d, r, take, off in row_parts(t * C_IN, C_IN, shard):
            w = wt[d, r:r + take, :]
            for row, col in spots[e]:
                at = ab * KB + row + off
                band[at:at + take, col:col + C_OUT] = w
    sy = shift_matrix(n, 1, 0)
    sz = shift_matrix(n, 0, 1)
    syz = shift_matrix(n, 1, 1)

    def move(s, v):
        return jnp.dot(s, v, preferred_element_type=f32).astype(bf16)

    for x in range(-1, BS):
        if x < 0:
            last = slice((BS - 1) * PLANE, BS * PLANE)
            plane = jnp.concatenate([rim[...], filled[:n - n // BX, last]], axis=0)
        else:
            plane = filled[:, x * PLANE:(x + 1) * PLANE]
        places_x = [(ox, x + 1 - 2 * ox) for ox in range(2) if 0 <= x + 1 - 2 * ox <= 2]
        for y in range(-1, BS):
            at = (y if y >= 0 else BS - 1) * ROW
            whole = plane[:, at:at + ROW]
            tail = plane[:, at + ROW - 128:at + ROW]
            if y < 0:
                whole, tail = move(sy, whole), move(syz, tail)
            else:
                tail = move(sz, tail)
            places_y = [(oy, y + 1 - 2 * oy) for oy in range(2) if 0 <= y + 1 - 2 * oy <= 2]
            for ox, a in places_x:
                for oy, b in places_y:
                    q = slice((ox * 2 + oy) * n, (ox * 2 + oy + 1) * n)
                    k = (a * 3 + b) * KB
                    cols[q, k:k + ROW] = whole
                    cols[q, k + ROW:k + KB] = tail
    for oz in range(2):
        v = jnp.dot(cols[...], band[:, oz * NB:(oz + 1) * NB], preferred_element_type=f32)[:, :C_OUT]
        s = 1.0 / (1.0 + jnp.exp(-v))
        act[oz] = (v * s).astype(bf16)
        slope = s * (1.0 + v * (1.0 - s))
        slopes[:, oz * NB:oz * NB + C_OUT] = (cot[oz].astype(f32) * slope).astype(bf16)
    for ab in range(9):
        g = lax.dot_general(cols[:, ab * KB:(ab + 1) * KB], slopes[...], (((0,), (0,)), ((), ())),
                            preferred_element_type=f32)
        for e in range(3):
            (r0, c0), (r1, c1) = spots[e]
            tap = g[r0:r0 + C_IN, c0:c0 + C_OUT] + g[r1:r1 + C_IN, c1:c1 + C_OUT]
            for d, r, take, off in row_parts((ab * 3 + e) * C_IN, C_IN, shard):
                left = max(0, min(take, cut - r))
                for start, length, base, lane in ((off, left, r, 0), (off + left, take - left, r + left - cut, C_OUT)):
                    if length:
                        for j, rr, tk, o2 in row_parts(base, length, piece):
                            terms[j, d, rr:rr + tk, lane:lane + C_OUT] = tap[start + o2:start + o2 + tk]


def layer(filled, rim, wt, cot, nb, nd, shard, cut, piece):
    rows = cot.shape[1]
    return pl.pallas_call(
        functools.partial(layer_kernel, nd, shard, cut, piece),
        out_shape=(
            jax.ShapeDtypeStruct(cot.shape, jnp.bfloat16),
            jax.ShapeDtypeStruct((nb, nd, piece, 2 * C_OUT), jnp.float32),
        ),
        scratch_shapes=[
            pltpu.VMEM((rows, 9 * KB), jnp.bfloat16),
            pltpu.VMEM((9 * KB, 2 * NB), jnp.bfloat16),
            pltpu.VMEM((rows, 2 * NB), jnp.bfloat16),
        ],
        compiler_params=pltpu.CompilerParams(vmem_limit_bytes=VMEM_LIMIT),
        name="layer",
    )(filled, rim, wt, cot)


def sum_kernel(nb, nd, shard, cut, piece, terms, out, give, got, pass_on, plane_in, down, down_in, final,
               s1, r1, s2, r2, s3, r3, s4, r4):
    f32, bf16 = jnp.float32, jnp.bfloat16
    nc = nb // 2
    me = lax.axis_index("brick")
    dp = lax.axis_index("dp")
    core = lax.rem(me, 2)
    chip = me // 2
    sib = me + 1 - 2 * core
    barrier = pltpu.get_barrier_semaphore()
    for k in range(1, nb):
        pl.semaphore_signal(barrier, inc=1, device_id={"brick": lax.rem(me + k, nb)}, device_id_type=MESH)
    for k in range(1, nd):
        pl.semaphore_signal(barrier, inc=1, device_id={"dp": lax.rem(dp + k, nd)}, device_id_type=MESH)
    pl.semaphore_wait(barrier, nb + nd - 2)
    sent = []
    for k in range(1, nc + 1):
        q = lax.rem(chip + k, nc)
        give[q] = terms[(1 - core) * nc + q].astype(bf16)
        c = copy_to(give.at[q], got.at[q], s1.at[k], r1.at[k], "brick", sib)
        c.start()
        sent.append(c)
    for k in range(1, nc):
        q = lax.rem(chip + k, nc)
        copy_to(give.at[q], got.at[q], s1.at[k], r1.at[k], "brick", sib).wait_recv()
        pass_on[k] = (terms[core * nc + q] + got[q].astype(f32)).astype(bf16)
        c = copy_to(pass_on.at[k], plane_in.at[k], s2.at[k], r2.at[k], "brick", q * 2 + core)
        c.start()
        sent.append(c)
    copy_to(give.at[chip], got.at[chip], s1.at[nc], r1.at[nc], "brick", sib).wait_recv()
    for k in range(1, nc):
        q = lax.rem(chip + nc - k, nc)
        copy_to(pass_on.at[k], plane_in.at[k], s2.at[k], r2.at[k], "brick", q * 2 + core).wait_recv()

    def plane_sum(d):
        total = terms[core * nc + chip, d] + got[chip, d].astype(f32)
        for k in range(1, nc):
            total = total + plane_in[k, d].astype(f32)
        return total

    for k in range(1, nd):
        o = lax.rem(dp + k, nd)
        down[k] = plane_sum(o).astype(bf16)
        c = copy_to(down.at[k], down_in.at[k], s3.at[k], r3.at[k], "dp", o)
        c.start()
        sent.append(c)
    total = plane_sum(dp)
    for k in range(1, nd):
        s = lax.rem(dp + nd - k, nd)
        copy_to(down.at[k], down_in.at[k], s3.at[k], r3.at[k], "dp", s).wait_recv()
        total = total + down_in[k].astype(f32)
    final[core * nc + chip] = total.astype(bf16)
    for k in range(1, nb):
        o = lax.rem(me + k, nb)
        slot = final.at[core * nc + chip]
        c = copy_to(slot, slot, s4.at[k], r4.at[k], "brick", o)
        c.start()
        sent.append(c)
    for k in range(1, nb):
        s = lax.rem(me + nb - k, nb)
        slot = final.at[lax.rem(s, 2) * nc + s // 2]
        copy_to(slot, slot, s4.at[k], r4.at[k], "brick", s).wait_recv()
    for j in range(nb):
        for rows, first, lane in ((cut, 0, 0), (shard - cut, cut, C_OUT)):
            take = min(piece, rows - j * piece)
            if take > 0:
                out[first + j * piece:first + j * piece + take, :] = (
                    final[j, :, lane:lane + C_OUT].astype(f32)[:take])
    for c in sent:
        c.wait_send()


def sum_terms(terms, nb, nd, shard, cut, piece):
    bf16 = jnp.bfloat16
    dma = pltpu.SemaphoreType.DMA
    nc = nb // 2
    wide = 2 * C_OUT
    return pl.pallas_call(
        functools.partial(sum_kernel, nb, nd, shard, cut, piece),
        out_shape=jax.ShapeDtypeStruct((shard, C_OUT), jnp.float32),
        scratch_shapes=[
            pltpu.VMEM((nc, nd, piece, wide), bf16),
            pltpu.VMEM((nc, nd, piece, wide), bf16),
            pltpu.VMEM((nc, nd, piece, wide), bf16),
            pltpu.VMEM((nc, nd, piece, wide), bf16),
            pltpu.VMEM((nd, piece, wide), bf16),
            pltpu.VMEM((nd, piece, wide), bf16),
            pltpu.VMEM((nb, piece, wide), bf16),
            dma((nc + 1,)), dma((nc + 1,)), dma((nc,)), dma((nc,)),
            dma((nd,)), dma((nd,)), dma((nb,)), dma((nb,)),
        ],
        compiler_params=pltpu.CompilerParams(
            collective_id=1, has_side_effects=True, vmem_limit_bytes=VMEM_LIMIT),
        name="sum_terms",
    )(terms)


def body(nb, nd, records, positions, weight, cotangent):
    cap = records.shape[2]
    shard = weight.shape[0]
    cut = up(-(-shard // 2), 8)
    piece = up(-(-cut // nb), 16)
    half = up(-(-shard // 2), 16)
    pos = jnp.pad(positions.reshape(nb, 1, cap), ((0, 0), (0, 7), (0, 128 - cap)))
    wt = jnp.pad(weight, ((0, 2 * half - shard), (0, 0)))
    arrived, places, full = exchange(records.reshape(records.shape[1:]), pos, wt, nb, nd)
    slots = nb * cap
    filled, edge = place(arrived.reshape(slots, -1), places[:, 0, :cap].reshape(1, slots))
    rim = lax.ppermute(edge, "brick", [(i, i + 1) for i in range(nb - 1)])
    shape7 = (BX, 2, BY, 2, BZ, 2, C_OUT)
    cot = cotangent.reshape(shape7).transpose(5, 1, 3, 0, 2, 4, 6).reshape(2, -1, C_OUT)
    act, terms = layer(filled, rim, full, cot, nb, nd, shard, cut, piece)
    act = act.reshape(2, 2, 2, BX, BY, BZ, C_OUT).transpose(3, 1, 4, 2, 5, 0, 6)
    return act.reshape(cotangent.shape), sum_terms(terms, nb, nd, shard, cut, piece)


def solution(mesh):
    placed = (
        P(("dp", "brick"), None, None, None),
        P(("dp", "brick"), None, None),
        P("dp", None),
        P("dp", "brick", None, None),
    )
    return jax.shard_map(
        functools.partial(body, mesh.shape["brick"], mesh.shape["dp"]),
        mesh=mesh,
        in_specs=placed,
        out_specs=(P("dp", "brick", None, None), P("dp", None)),
        check_vma=False,
    )
```

time: 236 us -> 71.9 us (0.30)
  the two profiles are of different devices: /device:TPU:25 before, /device:TPU:0 now
where the time goes in v1:
time: 71.9 us; the launch traced here: 71.5 us
  Pallas kernels  53.5 us (74%)
  local copies, waits for them, and re-layouts  13.5 us (19%)
  starting transfers between devices  3.74 us (5%)
    pallas_call x1, Pallas kernels, exchange(): pl.pallas_call(functools.partial(exchange_kernel, nb, nd, half), out_shap...  23 us
    pallas_call x1, Pallas kernels, sum_terms(): pl.pallas_call(functools.partial(sum_kernel, nb, nd, shard, cut, piece),...  21.8 us
    pallas_call x1, Pallas kernels, layer(): pl.pallas_call(functools.partial(layer_kernel, nd, shard, cut, piece), ou...  8.07 us
    unnamed x8, local copies, waits for them, and re-layouts  5.28 us
    ppermute x1, starting transfers between devices, body(): rim = lax.ppermute(edge, 'brick', [(i, i + 1) for i in range(nb - 1)])  3.74 us
    reshape x2, local copies, waits for them, and re-layouts, body(): cotangent.reshape(shape7).transpose(5, 1, 3, 0, 2, 4, 6)  3.51 us
  transfers between devices with their start and end apart: 1, of which 0 were waited for; matrix products, arithmetic and copies ran while one was open for 5% of the time, Pallas kernels for 0%

profile of v1, /device:TPU:0, one launch (start us, length us, event | category | flops | bytes accessed | tf_op | source)
XLA Modules:
  0.0 71.5 jit_solution(11572267334783939208)
XLA Ops:
  0.6 1.1 %copy.7 = bf16[648,192]{1,0:T(8,128)(2,1)S(1)} copy(bf16[648,192]{0,1:T(8,128)(2,1)} %param.6) | data formatting | bytes 497664 | tf_op args[2]
  1.8 1.3 %pad.8.pos = s32[8,8,128]{2,1,0:T(8,128)} pad(s32[8,1,16]{2,1,0:T(1,128)} %bitcast.17, s32[]{:T(128)} %constant.2.clone.1), padding=0_0x0_7x0_112 | pad | bytes 33284 | tf_op jit(solution)/shard_map/jit(_pad)/pad | solution.py:340
  3.1 0.8 %pad.9.wt = bf16[672,192]{1,0:T(8,128)(2,1)} pad(bf16[648,192]{1,0:T(8,128)(2,1)S(1)} %copy.7, bf16[]{:T(256)} %constant.3.clone.1), padding=0_24x0_0 | pad | bytes 506882 | tf_op jit(solution)/shard_map/jit(_pad)/pad | solution.py:341
  3.9 23.0 %exchange.1 = (bf16[8,16,6144]{2,1,0:T(8,128)(2,1)}, s32[8,8,128]{2,1,0:T(8,128)}, bf16[4,672,192]{2,1,0:T(8,128)(2,1)}) custom-call(bf16[8,16,6144]{2,1,0:T(8,128)(2,1)} %bitcast.16, s32[8,8,128]{2,1,0:T(8,128)} %pad.8.pos, bf16[672,192]{1,0:T(8,128)(2,1)} %pad.9.wt), custom_call_target="tpu_custom_call" | custom-call | tf_op jit(solution)/shard_map/exchange/pallas_call | solution.py:93
  26.9 0.8 %slice_reduce_fusion = s32[8,16]{1,0:T(8,128)S(1)} fusion(s32[8,8,128]{2,1,0:T(8,128)} %get-tuple-element.10), kind=kLoop, calls=%fused_computation | loop fusion | bytes 1024 | tf_op jit(solution)/shard_map/slice | solution.py:344
  27.6 0.1 reshape_squeeze.3.places
  27.7 0.0 copy-start.1
  27.7 1.4 %copy-done.1 = bf16[8,16,6144]{2,1,0:T(8,128)(2,1)S(1)} copy-done((bf16[8,16,6144]{2,1,0:T(8,128)(2,1)S(1)}, bf16[8,16,6144]{2,1,0:T(8,128)(2,1)}, u32[]{:S(2)}) %copy-start.1) | copy-done | bytes 1572888
  29.1 0.0 copy-start.2
  29.1 0.6 place.1
  29.7 3.7 %collective-permute-start = (bf16[64,1536]{1,0:T(8,128)(2,1)S(1)}, bf16[64,1536]{1,0:T(8,128)(2,1)S(1)}, u32[]{:S(2)}, u32[]{:S(2)}) collective-permute-start(bf16[64,1536]{1,0:T(8,128)(2,1)S(1)} %get-tuple-element.12), channel_id=1, source_target_pairs={{0,1},{1,2},{2,3},{3,4},{4,5},{5,6},{6,7},{8,9},{9,10},{10,11},{11... | collective-permute-start | bytes 589832 | tf_op jit(solution)/shard_map/ppermute | solution.py:345
  33.4 2.4 %reshape.28 = bf16[2,2,8,2,8,2,192]{6,5,4,3,2,1,0:T(2,128)(2,1)} reshape(bf16[1,4,16,3072]{3,2,1,0:T(8,128)(2,1)} %param.7) | data formatting | bytes 786432 | tf_op jit(solution)/shard_map/reshape | solution.py:347
  35.8 1.1 %copy.8 = bf16[2,2,8,2,8,2,192]{6,4,2,0,3,1,5:T(8,128)(2,1)S(1)} copy(bf16[2,2,8,2,8,2,192]{6,5,4,3,2,1,0:T(2,128)(2,1)} %reshape.28) | data formatting | bytes 786432 | tf_op jit(solution)/shard_map/reshape | solution.py:347
  37.0 0.0 collective-permute-done.rim
  37.0 0.0 copy-done.2
  37.0 8.1 %layer.1 = (bf16[2,512,192]{2,1,0:T(8,128)(2,1)S(1)}, f32[8,4,48,384]{3,2,1,0:T(8,128)}) custom-call(bf16[128,6144]{1,0:T(8,128)(2,1)S(1)} %get-tuple-element.11.filled, bf16[64,1536]{1,0:T(8,128)(2,1)S(1)} %collective-permute-done.rim, bf16[4,672,192]{2,1,0:T(8,128)(2,1)S(1)} %copy-done.2, bf16[2,512,192]{2,1,0:T(8,128)(2,1)S(1)} %bitcast.13), custom_call_target="tpu_custom_call" | custom-call | tf_op jit(solution)/shard_map/layer/pallas_call | solution.py:221
  45.0 0.5 copy.9
  45.6 1.3 %reshape.31 = bf16[1,4,16,3072]{3,2,1,0:T(8,128)(2,1)} reshape(bf16[2,2,8,2,8,2,192]{6,5,4,3,2,1,0:T(2,128)(2,1)S(1)} %copy.9) | data formatting | bytes 786432 | tf_op jit(solution)/shard_map/reshape | solution.py:350
  46.9 0.0 copy-start
  46.9 1.7 %copy-done = f32[8,4,48,384]{3,2,1,0:T(8,128)S(1)} copy-done((f32[8,4,48,384]{3,2,1,0:T(8,128)S(1)}, f32[8,4,48,384]{3,2,1,0:T(8,128)}, u32[]{:S(2)}) %copy-start) | copy-done | bytes 2359320
  48.5 21.8 %sum_terms.1 = f32[648,192]{1,0:T(8,128)S(1)} custom-call(f32[8,4,48,384]{3,2,1,0:T(8,128)S(1)} %copy-done), custom_call_target="tpu_custom_call" | custom-call | tf_op jit(solution)/shard_map/sum_terms/pallas_call | solution.py:314
  70.4 1.1 %copy.10 = f32[648,192]{0,1:T(8,128)} copy(f32[648,192]{1,0:T(8,128)S(1)} %sum_terms.1) | data formatting | bytes 995328
Async XLA Ops:
  27.7 1.4 %copy-start.1 = (bf16[8,16,6144]{2,1,0:T(8,128)(2,1)S(1)}, bf16[8,16,6144]{2,1,0:T(8,128)(2,1)}, u32[]{:S(2)}) copy-start(bf16[8,16,6144]{2,1,0:T(8,128)(2,1)} %get-tuple-element.9) | copy-start | bytes 4718596
  29.1 7.9 %copy-start.2 = (bf16[4,672,192]{2,1,0:T(8,128)(2,1)S(1)}, bf16[4,672,192]{2,1,0:T(8,128)(2,1)}, u32[]{:S(2)}) copy-start(bf16[4,672,192]{2,1,0:T(8,128)(2,1)} %get-tuple-element.13.wt) | copy-start | bytes 3096580
  29.7 7.3 %collective-permute-start = (bf16[64,1536]{1,0:T(8,128)(2,1)S(1)}, bf16[64,1536]{1,0:T(8,128)(2,1)S(1)}, u32[]{:S(2)}, u32[]{:S(2)}) collective-permute-start(bf16[64,1536]{1,0:T(8,128)(2,1)S(1)} %get-tuple-element.12), channel_id=1, source_target_pairs={{0,1},{1,2},{2,3},{3,4},{4,5},{5,6},{6,7},{8,9},{9,10},{10,11},{11... | collective-permute-start | bytes 589832 | tf_op jit(solution)/shard_map/ppermute | solution.py:345
  46.9 1.7 %copy-start = (f32[8,4,48,384]{3,2,1,0:T(8,128)S(1)}, f32[8,4,48,384]{3,2,1,0:T(8,128)}, u32[]{:S(2)}) copy-start(f32[8,4,48,384]{3,2,1,0:T(8,128)} %get-tuple-element.15.terms) | copy-start | bytes 7077892

commit v2 on v1

--- a/solution.py
+++ b/solution.py
@@ -234,7 +234,7 @@
     )(filled, rim, wt, cot)
 
 
-def sum_kernel(nb, nd, shard, cut, piece, terms, out, give, got, pass_on, plane_in, down, down_in, final,
+def sum_kernel(nb, nd, shard, cut, piece, terms, out, got, pass_on, plane_in, down, down_in, final,
                s1, r1, s2, r2, s3, r3, s4, r4):
     f32, bf16 = jnp.float32, jnp.bfloat16
     nc = nb // 2
@@ -252,24 +252,23 @@
     sent = []
     for k in range(1, nc + 1):
         q = lax.rem(chip + k, nc)
-        give[q] = terms[(1 - core) * nc + q].astype(bf16)
-        c = copy_to(give.at[q], got.at[q], s1.at[k], r1.at[k], "brick", sib)
+        c = copy_to(terms.at[(1 - core) * nc + q], got.at[q], s1.at[k], r1.at[k], "brick", sib)
         c.start()
         sent.append(c)
     for k in range(1, nc):
         q = lax.rem(chip + k, nc)
-        copy_to(give.at[q], got.at[q], s1.at[k], r1.at[k], "brick", sib).wait_recv()
-        pass_on[k] = (terms[core * nc + q] + got[q].astype(f32)).astype(bf16)
+        copy_to(terms.at[q], got.at[q], s1.at[k], r1.at[k], "brick", sib).wait_recv()
+        pass_on[k] = (terms[core * nc + q] + got[q]).astype(bf16)
         c = copy_to(pass_on.at[k], plane_in.at[k], s2.at[k], r2.at[k], "brick", q * 2 + core)
         c.start()
         sent.append(c)
-    copy_to(give.at[chip], got.at[chip], s1.at[nc], r1.at[nc], "brick", sib).wait_recv()
+    copy_to(terms.at[chip], got.at[chip], s1.at[nc], r1.at[nc], "brick", sib).wait_recv()
     for k in range(1, nc):
         q = lax.rem(chip + nc - k, nc)
         copy_to(pass_on.at[k], plane_in.at[k], s2.at[k], r2.at[k], "brick", q * 2 + core).wait_recv()
 
     def plane_sum(d):
-        total = terms[core * nc + chip, d] + got[chip, d].astype(f32)
+        total = terms[core * nc + chip, d] + got[chip, d]
         for k in range(1, nc):
             total = total + plane_in[k, d].astype(f32)
         return total
@@ -285,7 +284,7 @@
         s = lax.rem(dp + nd - k, nd)
         copy_to(down.at[k], down_in.at[k], s3.at[k], r3.at[k], "dp", s).wait_recv()
         total = total + down_in[k].astype(f32)
-    final[core * nc + chip] = total.astype(bf16)
+    final[core * nc + chip] = total
     for k in range(1, nb):
         o = lax.rem(me + k, nb)
         slot = final.at[core * nc + chip]
@@ -301,7 +300,7 @@
             take = min(piece, rows - j * piece)
             if take > 0:
                 out[first + j * piece:first + j * piece + take, :] = (
-                    final[j, :, lane:lane + C_OUT].astype(f32)[:take])
+                    final[j, :take, lane:lane + C_OUT])
     for c in sent:
         c.wait_send()
 
@@ -315,13 +314,12 @@
         functools.partial(sum_kernel, nb, nd, shard, cut, piece),
         out_shape=jax.ShapeDtypeStruct((shard, C_OUT), jnp.float32),
         scratch_shapes=[
-            pltpu.VMEM((nc, nd, piece, wide), bf16),
-            pltpu.VMEM((nc, nd, piece, wide), bf16),
+            pltpu.VMEM((nc, nd, piece, wide), jnp.float32),
             pltpu.VMEM((nc, nd, piece, wide), bf16),
             pltpu.VMEM((nc, nd, piece, wide), bf16),
             pltpu.VMEM((nd, piece, wide), bf16),
             pltpu.VMEM((nd, piece, wide), bf16),
-            pltpu.VMEM((nb, piece, wide), bf16),
+            pltpu.VMEM((nb, piece, wide), jnp.float32),
             dma((nc + 1,)), dma((nc + 1,)), dma((nc,)), dma((nc,)),
             dma((nd,)), dma((nd,)), dma((nb,)), dma((nb,)),
         ],
@@ -331,7 +329,7 @@
     )(terms)
 
 
-def body(nb, nd, records, positions, weight, cotangent):
+def staged(nb, nd, records, positions, weight, cotangent):
     cap = records.shape[2]
     shard = weight.shape[0]
     cut = up(-(-shard // 2), 8)
@@ -350,6 +348,316 @@
     return act.reshape(cotangent.shape), sum_terms(terms, nb, nd, shard, cut, piece)
 
 
+def fused_kernel(nb, nd, cap, shard, cut, piece, rec, pos, wt, cot, act_out, grad_out,
+                 stage, spread, arrived, wts, filled, rim, cols, band, slopes, cots, acts,
+                 terms, got, pass_on, plane_in, down, down_in, own, final, grad,
+                 rs, rr, ps, pr, ws, wr, xs, xr, loc, bs, br, s1, r1, s2, r2, s3, r3, s4, r4, s5, r5):
+    f32, bf16 = jnp.float32, jnp.bfloat16
+    n = BX * BY * BZ
+    nc = nb // 2
+    me = lax.axis_index("brick")
+    dp = lax.axis_index("dp")
+    core = lax.rem(me, 2)
+    chip = me // 2
+    sib = me + 1 - 2 * core
+    barrier = pltpu.get_barrier_semaphore()
+    for k in range(1, nb):
+        pl.semaphore_signal(barrier, inc=1, device_id={"brick": lax.rem(me + k, nb)}, device_id_type=MESH)
+    for k in range(1, nd):
+        pl.semaphore_signal(barrier, inc=1, device_id={"dp": lax.rem(dp + k, nd)}, device_id_type=MESH)
+    local = [
+        pltpu.make_async_copy(rec.at[me], arrived.at[me], loc.at[0]),
+        pltpu.make_async_copy(wt, wts.at[dp], loc.at[1]),
+    ]
+    for c in local:
+        c.start()
+    lane = lax.broadcasted_iota(jnp.int32, (cap, nb * cap), 1)
+    slot = lax.broadcasted_iota(jnp.int32, (cap, nb * cap), 0)
+    to_lanes = jnp.where(lane == slot + me * cap, 1.0, 0.0).astype(bf16)
+    lined = jnp.dot(pos[...].astype(f32).astype(bf16), to_lanes, preferred_element_type=f32)
+    for o in range(nb):
+        stage[o] = jnp.broadcast_to(lined[o:o + 1], stage.shape[1:])
+    pl.semaphore_wait(barrier, nb + nd - 2)
+    half = wt.shape[0] // 2
+    mine = pl.ds(pl.multiple_of(core * half, 16), half)
+    theirs = pl.ds(pl.multiple_of((1 - core) * half, 16), half)
+    sent = []
+
+    def go(c):
+        c.start()
+        sent.append(c)
+
+    for k in range(1, nd):
+        o = lax.rem(dp + k, nd)
+        go(copy_to(wt.at[mine], wts.at[dp, mine], ws.at[k], wr.at[k], "dp", o))
+    for k in range(1, nb):
+        o = lax.rem(me + k, nb)
+        go(copy_to(stage.at[o], spread.at[me], ps.at[k], pr.at[k], "brick", o))
+        go(copy_to(rec.at[o], arrived.at[me], rs.at[k], rr.at[k], "brick", o))
+    band[...] = jnp.zeros_like(band)
+    slopes[...] = jnp.zeros_like(slopes)
+    terms[...] = jnp.zeros_like(terms)
+    rows = 4 * n
+    strip = 4 * BX * BY
+    pair = 2 * C_OUT
+
+    def home(r):
+        bz, i, j = r // strip, lax.rem(r // (2 * BY), 2 * BX), lax.rem(r, 2 * BY)
+        q = lax.rem(i, 2) * 2 + lax.rem(j, 2)
+        return q * n + (i // 2) * (BY * BZ) + (j // 2) * BZ + bz
+
+    r_id = lax.broadcasted_iota(jnp.int32, (rows, rows), 0)
+    c_id = lax.broadcasted_iota(jnp.int32, (rows, rows), 1)
+    turn = jnp.where(r_id == home(c_id), 1.0, 0.0).astype(bf16)
+    lined_cot = jnp.concatenate(
+        [cot[:, :, z * pair:(z + 1) * pair].reshape(strip, pair) for z in range(BZ)], axis=0)
+    turned = jnp.dot(turn, lined_cot, preferred_element_type=f32)
+    cots[0] = turned[:, :C_OUT]
+    cots[1] = turned[:, C_OUT:]
+    for k in range(1, nd):
+        s = lax.rem(dp + nd - k, nd)
+        copy_to(wt.at[mine], wts.at[s, mine], ws.at[k], wr.at[k], "dp", s).wait_recv()
+        go(copy_to(wts.at[s, mine], wts.at[s, mine], xs.at[k], xr.at[k], "brick", sib))
+    for k in range(1, nd):
+        s = lax.rem(dp + nd - k, nd)
+        copy_to(wt.at[theirs], wts.at[s, theirs], xs.at[k], xr.at[k], "brick", sib).wait_recv()
+    local[1].wait()
+    spots = {0: ((KB - C_IN, 0), (C_IN, NB)), 1: ((0, 0), (2 * C_IN, NB)), 2: ((C_IN, 0), (3 * C_IN, NB))}
+    for d in range(nd):
+        w = wts[d].astype(f32).T.astype(bf16)
+        for t in range(TAPS):
+            ab, e = divmod(t, 3)
+            for d2, r, take, off in row_parts(t * C_IN, C_IN, shard):
+                if d2 == d:
+                    for row, col in spots[e]:
+                        at = ab * KB + row + off
+                        band[at:at + take, col:col + C_OUT] = w[r:r + take]
+    sy = shift_matrix(n, 1, 0)
+    sz = shift_matrix(n, 0, 1)
+    syz = shift_matrix(n, 1, 1)
+    for k in range(1, nb):
+        s = lax.rem(me + nb - k, nb)
+        copy_to(stage.at[s], spread.at[s], ps.at[k], pr.at[k], "brick", s).wait_recv()
+    spread[me] = stage[me]
+    for k in range(1, nb):
+        s = lax.rem(me + nb - k, nb)
+        copy_to(rec.at[s], arrived.at[s], rs.at[k], rr.at[k], "brick", s).wait_recv()
+    local[0].wait()
+    held = spread[0]
+    for s in range(1, nb):
+        held = held + spread[s]
+    want = lax.broadcasted_iota(jnp.int32, (n, nb * cap), 0).astype(f32)
+    pick = jnp.where(held[0:1] == want, 1.0, 0.0).astype(bf16)
+
+    def place_plane(x):
+        lanes = slice(x * PLANE, (x + 1) * PLANE)
+        records = arrived[:, :, lanes].reshape(nb * cap, PLANE)
+        filled[:, lanes] = jnp.dot(pick, records, preferred_element_type=f32).astype(bf16)
+
+    last = slice((BS - 1) * PLANE, BS * PLANE)
+    place_plane(BS - 1)
+    edge = copy_to(filled.at[n - n // BX:n, last], rim, bs, br, "brick", lax.rem(me + 1, nb))
+    pl.when(me < nb - 1)(edge.start)
+    for x in range(BS - 1):
+        place_plane(x)
+
+    def move(s, v):
+        return jnp.dot(s, v, preferred_element_type=f32).astype(bf16)
+
+    def fill_columns(x, plane):
+        for y in range(-1, BS):
+            at = (y if y >= 0 else BS - 1) * ROW
+            whole = plane[:, at:at + ROW]
+            tail = plane[:, at + ROW - 128:at + ROW]
+            if y < 0:
+                whole, tail = move(sy, whole), move(syz, tail)
+            else:
+                tail = move(sz, tail)
+            for ox in range(2):
+                a = x + 1 - 2 * ox
+                for oy in range(2):
+                    b = y + 1 - 2 * oy
+                    if 0 <= a <= 2 and 0 <= b <= 2:
+                        q = slice((ox * 2 + oy) * n, (ox * 2 + oy + 1) * n)
+                        k = (a * 3 + b) * KB
+                        cols[q, k:k + ROW] = whole
+                        cols[q, k + ROW:k + KB] = tail
+
+    def forward(ox):
+        q = slice(ox * 2 * n, (ox + 1) * 2 * n)
+        for oz in range(2):
+            v = jnp.dot(cols[q, :], band[:, oz * NB:(oz + 1) * NB], preferred_element_type=f32)[:, :C_OUT]
+            s = 1.0 / (1.0 + jnp.exp(-v))
+            acts[q, oz * C_OUT:(oz + 1) * C_OUT] = v * s
+            slope = s * (1.0 + v * (1.0 - s))
+            slopes[q, oz * NB:oz * NB + C_OUT] = (cots[oz, q, :] * slope).astype(bf16)
+
+    for x in range(BS):
+        fill_columns(x, filled[:, x * PLANE:(x + 1) * PLANE])
+    forward(1)
+
+    @pl.when(me > 0)
+    def _():
+        edge.wait_recv()
+
+    @pl.when(me == 0)
+    def _():
+        rim[...] = jnp.zeros_like(rim)
+
+    fill_columns(-1, jnp.concatenate([rim[...], filled[:n - n // BX, last]], axis=0))
+    forward(0)
+
+    def tap_rows(ab):
+        g = lax.dot_general(cols[:, ab * KB:(ab + 1) * KB], slopes[...], (((0,), (0,)), ((), ())),
+                            preferred_element_type=f32)
+        for e in range(3):
+            (r0, c0), (r1, c1) = spots[e]
+            tap = g[r0:r0 + C_IN, c0:c0 + C_OUT] + g[r1:r1 + C_IN, c1:c1 + C_OUT]
+            for d, r, take, off in row_parts((ab * 3 + e) * C_IN, C_IN, shard):
+                left = max(0, min(take, cut - r))
+                for start, length, base, at in ((off, left, r, 0), (off + left, take - left, r + left - cut, C_OUT)):
+                    if length:
+                        for j, row, tk, o2 in row_parts(base, length, piece):
+                            terms[d, j, row:row + tk, at:at + C_OUT] = tap[start + o2:start + o2 + tk]
+
+    def to_sibling(d):
+        return copy_to(terms.at[d, pl.ds((1 - core) * nc, nc)], got.at[d], s1.at[d], r1.at[d], "brick", sib)
+
+    def to_chips(d):
+        to_sibling(d).wait_recv()
+        for k in range(1, nc):
+            q = lax.rem(chip + k, nc)
+            pass_on[d, k] = (terms[d, core * nc + q] + got[d, q]).astype(bf16)
+            go(copy_to(pass_on.at[d, k], plane_in.at[d, k], s2.at[d, k], r2.at[d, k], "brick", q * 2 + core))
+
+    def to_rank(d):
+        total = terms[d, core * nc + chip] + got[d, chip]
+        for k in range(1, nc):
+            q = lax.rem(chip + nc - k, nc)
+            copy_to(pass_on.at[d, k], plane_in.at[d, k], s2.at[d, k], r2.at[d, k], "brick", q * 2 + core).wait_recv()
+            total = total + plane_in[d, k].astype(f32)
+
+        @pl.when(dp == d)
+        def _():
+            own[...] = total
+
+        @pl.when(dp != d)
+        def _():
+            down[d] = total.astype(bf16)
+            copy_to(down.at[d], down_in.at[dp], s3.at[d], r3.at[dp], "dp", d).start()
+
+    ready = 0
+    for ab in range(9):
+        tap_rows(ab)
+        while ready < nd and (ready + 1) * shard <= (ab + 1) * 3 * C_IN:
+            go(to_sibling(ready))
+            if ready:
+                to_chips(ready - 1)
+            ready += 1
+    to_chips(nd - 1)
+    shown = lax.dot_general(turn, acts[...].astype(bf16), (((0,), (0,)), ((), ())), preferred_element_type=f32)
+    for z in range(BZ):
+        act_out[:, :, z * pair:(z + 1) * pair] = (
+            shown[z * strip:(z + 1) * strip].astype(bf16).reshape(2 * BX, 2 * BY, pair))
+    for d in range(nd):
+        to_rank(d)
+    total = own[...]
+    for k in range(1, nd):
+        s = lax.rem(dp + nd - k, nd)
+        copy_to(down.at[s], down_in.at[s], s3.at[s], r3.at[s], "dp", s).wait_recv()
+        total = total + down_in[s].astype(f32)
+    here = core * nc + chip
+    final[here] = total
+    for k in range(1, nc):
+        q = lax.rem(chip + k, nc)
+        go(copy_to(final.at[here], final.at[here], s4.at[k], r4.at[k], "brick", q * 2 + core))
+    go(copy_to(final.at[here], final.at[here], s5.at[0], r5.at[0], "brick", sib))
+    for k in range(1, nc):
+        q = lax.rem(chip + nc - k, nc)
+        there = final.at[core * nc + q]
+        copy_to(there, there, s4.at[k], r4.at[k], "brick", q * 2 + core).wait_recv()
+        go(copy_to(there, there, s5.at[k], r5.at[k], "brick", sib))
+    for k in range(nc):
+        q = lax.rem(chip + nc - k, nc)
+        there = final.at[(1 - core) * nc + q]
+        copy_to(there, there, s5.at[k], r5.at[k], "brick", sib).wait_recv()
+    for j in range(nb):
+        for count, first, at in ((cut, 0, 0), (shard - cut, cut, C_OUT)):
+            take = min(piece, count - j * piece)
+            if take > 0:
+                grad[first + j * piece:first + j * piece + take, :] = final[j, :take, at:at + C_OUT]
+    grad_out[...] = grad[...].T
+    for c in sent:
+        c.wait_send()
+    pl.when(me < nb - 1)(edge.wait_send)
+    for d in range(nd):
+        @pl.when(dp != d)
+        def _():
+            copy_to(down.at[d], down_in.at[dp], s3.at[d], r3.at[dp], "dp", d).wait_send()
+
+
+def fused(nb, nd, records, positions, weight, cotangent):
+    cap = records.shape[2]
+    shard = weight.shape[0]
+    cut = up(-(-shard // 2), 8)
+    piece = up(-(-cut // nb), 16)
+    f32, bf16 = jnp.float32, jnp.bfloat16
+    n = BX * BY * BZ
+    nc = nb // 2
+    wide = 2 * C_OUT
+    dma = pltpu.SemaphoreType.DMA
+    vmem = pltpu.VMEM
+    act, grad = pl.pallas_call(
+        functools.partial(fused_kernel, nb, nd, cap, shard, cut, piece),
+        out_shape=(
+            jax.ShapeDtypeStruct(cotangent.shape[1:], bf16),
+            jax.ShapeDtypeStruct((C_OUT, shard), f32),
+        ),
+        in_specs=[
+            pl.BlockSpec(memory_space=pl.ANY),
+            pl.BlockSpec(memory_space=pltpu.VMEM),
+            pl.BlockSpec(memory_space=pltpu.VMEM),
+            pl.BlockSpec(memory_space=pltpu.VMEM),
+        ],
+        scratch_shapes=[
+            vmem((nb, 8, nb * cap), f32),
+            vmem((nb, 8, nb * cap), f32),
+            vmem(records.shape[1:], bf16),
+            vmem((nd, C_OUT, shard), bf16),
+            vmem((n, BS * PLANE), bf16),
+            vmem((n // BX, PLANE), bf16),
+            vmem((4 * n, 9 * KB), bf16),
+            vmem((9 * KB, 2 * NB), bf16),
+            vmem((4 * n, 2 * NB), bf16),
+            vmem((2, 4 * n, C_OUT), f32),
+            vmem((4 * n, wide), f32),
+            vmem((nd, nb, piece, wide), f32),
+            vmem((nd, nc, piece, wide), f32),
+            vmem((nd, nc, piece, wide), bf16),
+            vmem((nd, nc, piece, wide), bf16),
+            vmem((nd, piece, wide), bf16),
+            vmem((nd, piece, wide), bf16),
+            vmem((piece, wide), f32),
+            vmem((nb, piece, wide), f32),
+            vmem((shard, C_OUT), f32),
+            dma((nb,)), dma((nb,)), dma((nb,)), dma((nb,)),
+            dma((nd,)), dma((nd,)), dma((nd,)), dma((nd,)), dma((2,)), dma, dma,
+            dma((nd,)), dma((nd,)), dma((nd, nc)), dma((nd, nc)),
+            dma((nd,)), dma((nd,)), dma((nc,)), dma((nc,)), dma((nc,)), dma((nc,)),
+        ],
+        compiler_params=pltpu.CompilerParams(
+            collective_id=2, has_side_effects=True, vmem_limit_bytes=VMEM_LIMIT),
+        name="fused",
+    )(records.reshape(records.shape[1:]), positions.reshape(nb, cap), weight.T,
+      cotangent.reshape(cotangent.shape[1:]))
+    return act.reshape(cotangent.shape), grad.T
+
+
+def body(nb, nd, records, positions, weight, cotangent):
+    path = staged if records.shape[2] % 16 else fused
+    return path(nb, nd, records, positions, weight, cotangent)
+
+
 def solution(mesh):
     placed = (
         P(("dp", "brick"), None, None, None),

time: 71.9 us -> 56.7 us (0.79)
  the two profiles are of different devices: /device:TPU:0 before, /device:TPU:25 now
where the time goes in v2:
time: 56.7 us; the launch traced here: 56.4 us
  Pallas kernels  50.2 us (89%)
  local copies, waits for them, and re-layouts  5.61 us (10%)
  between operations  0.65 us (1%)
    pallas_call x1, Pallas kernels, fused(): pl.pallas_call(functools.partial(fused_kernel, nb, nd, cap, shard, cut, p...  50.2 us
    unnamed x10, local copies, waits for them, and re-layouts  5.61 us

profile of v2, /device:TPU:25, one launch (start us, length us, event | category | flops | bytes accessed | tf_op | source)
XLA Modules:
  0.0 56.4 jit_solution(7039093378790393677)
XLA Ops:
  0.6 0.0 copy-start
  0.6 1.4 %copy-done = bf16[1,8,16,6144]{3,2,1,0:T(8,128)(2,1)S(1)} copy-done((bf16[1,8,16,6144]{3,2,1,0:T(8,128)(2,1)S(1)}, bf16[1,8,16,6144]{3,2,1,0:T(8,128)(2,1)}, u32[]{:S(2)}) %copy-start) | copy-done | bytes 1572888
  2.0 0.0 copy-start.1
  2.0 1.0 %copy-done.1 = bf16[1,4,16,3072]{3,2,1,0:T(8,128)(2,1)S(1)} copy-done((bf16[1,4,16,3072]{3,2,1,0:T(8,128)(2,1)S(1)}, bf16[1,4,16,3072]{3,2,1,0:T(8,128)(2,1)}, u32[]{:S(2)}) %copy-start.1) | copy-done | bytes 393240
  3.0 0.0 copy-start.2
  3.0 1.0 %copy-done.2 = bf16[648,192]{0,1:T(8,128)(2,1)S(1)} copy-done((bf16[648,192]{0,1:T(8,128)(2,1)S(1)}, bf16[648,192]{0,1:T(8,128)(2,1)}, u32[]{:S(2)}) %copy-start.2) | copy-done | bytes 248856
  4.0 0.0 copy-start.3
  4.0 0.7 %copy-done.3 = s32[1,8,16]{2,1,0:T(8,128)S(1)} copy-done((s32[1,8,16]{2,1,0:T(8,128)S(1)}, s32[1,8,16]{2,1,0:T(8,128)}, u32[]{:S(2)}) %copy-start.3) | copy-done | bytes 536
  4.7 50.2 %fused.1 = (bf16[4,16,3072]{2,1,0:T(8,128)(2,1)S(1)}, f32[192,648]{1,0:T(8,128)S(1)}) custom-call(bf16[8,16,6144]{2,1,0:T(8,128)(2,1)S(1)} %bitcast.6, s32[8,16]{1,0:T(8,128)S(1)} %bitcast.11, bf16[192,648]{1,0:T(8,128)(2,1)S(1)} %bitcast.10, bf16[4,16,3072]{2,1,0:T(8,128)(2,1)S(1)} %bitcast.9), custom_call_target="tpu_custom_call" | custom-call | tf_op jit(solution)/shard_map/fused/pallas_call | solution.py:610
  54.9 0.7 %copy.8 = bf16[1,4,16,3072]{3,2,1,0:T(8,128)(2,1)} copy(bf16[1,4,16,3072]{3,2,1,0:T(8,128)(2,1)S(1)} %bitcast.8) | data formatting | bytes 786432
  55.6 0.8 %copy.9 = f32[648,192]{0,1:T(8,128)} copy(f32[648,192]{0,1:T(8,128)S(1)} %bitcast.7) | data formatting | bytes 995328
Async XLA Ops:
  0.6 1.4 %copy-start = (bf16[1,8,16,6144]{3,2,1,0:T(8,128)(2,1)S(1)}, bf16[1,8,16,6144]{3,2,1,0:T(8,128)(2,1)}, u32[]{:S(2)}) copy-start(bf16[1,8,16,6144]{3,2,1,0:T(8,128)(2,1)} %param.4) | copy-start | bytes 4718596
  2.0 1.0 %copy-start.1 = (bf16[1,4,16,3072]{3,2,1,0:T(8,128)(2,1)S(1)}, bf16[1,4,16,3072]{3,2,1,0:T(8,128)(2,1)}, u32[]{:S(2)}) copy-start(bf16[1,4,16,3072]{3,2,1,0:T(8,128)(2,1)} %param.7) | copy-start | bytes 1179652
  3.0 1.0 %copy-start.2 = (bf16[648,192]{0,1:T(8,128)(2,1)S(1)}, bf16[648,192]{0,1:T(8,128)(2,1)}, u32[]{:S(2)}) copy-start(bf16[648,192]{0,1:T(8,128)(2,1)} %param.6) | copy-start | bytes 746500
  4.0 0.7 %copy-start.3 = (s32[1,8,16]{2,1,0:T(8,128)S(1)}, s32[1,8,16]{2,1,0:T(8,128)}, u32[]{:S(2)}) copy-start(s32[1,8,16]{2,1,0:T(8,128)} %param.5) | copy-start | bytes 1540

commit v3 on v2

--- a/solution.py
+++ b/solution.py
@@ -20,6 +20,7 @@
 NB = 256
 MESH = pl.DeviceIdType.MESH
 VMEM_LIMIT = 48 * 1024 * 1024
+FUSED_LIMIT = 62 * 1024 * 1024
 
 
 def up(n, k):
@@ -348,8 +349,8 @@
     return act.reshape(cotangent.shape), sum_terms(terms, nb, nd, shard, cut, piece)
 
 
-def fused_kernel(nb, nd, cap, shard, cut, piece, rec, pos, wt, cot, act_out, grad_out,
-                 stage, spread, arrived, wts, filled, rim, cols, band, slopes, cots, acts,
+def fused_kernel(nb, nd, cap, shard, cut, piece, rec, pos_in, wt_in, cot_in, act_hbm, grad_out,
+                 act_out, pos, wt, cot, linear, stage, spread, arrived, wts, filled, rim, cols, band, slopes, cots, acts,
                  terms, got, pass_on, plane_in, down, down_in, own, final, grad,
                  rs, rr, ps, pr, ws, wr, xs, xr, loc, bs, br, s1, r1, s2, r2, s3, r3, s4, r4, s5, r5):
     f32, bf16 = jnp.float32, jnp.bfloat16
@@ -367,10 +368,14 @@
         pl.semaphore_signal(barrier, inc=1, device_id={"dp": lax.rem(dp + k, nd)}, device_id_type=MESH)
     local = [
         pltpu.make_async_copy(rec.at[me], arrived.at[me], loc.at[0]),
-        pltpu.make_async_copy(wt, wts.at[dp], loc.at[1]),
+        pltpu.make_async_copy(wt_in, wts.at[dp], loc.at[1]),
+        pltpu.make_async_copy(cot_in, cot, loc.at[2]),
+        pltpu.make_async_copy(wt_in, wt, loc.at[3]),
+        pltpu.make_async_copy(pos_in, pos, loc.at[4]),
     ]
-    for c in local:
-        c.start()
+    for c in reversed(local):
+        c.start()
+    local[4].wait()
     lane = lax.broadcasted_iota(jnp.int32, (cap, nb * cap), 1)
     slot = lax.broadcasted_iota(jnp.int32, (cap, nb * cap), 0)
     to_lanes = jnp.where(lane == slot + me * cap, 1.0, 0.0).astype(bf16)
@@ -378,6 +383,7 @@
     for o in range(nb):
         stage[o] = jnp.broadcast_to(lined[o:o + 1], stage.shape[1:])
     pl.semaphore_wait(barrier, nb + nd - 2)
+    local[3].wait()
     half = wt.shape[0] // 2
     mine = pl.ds(pl.multiple_of(core * half, 16), half)
     theirs = pl.ds(pl.multiple_of((1 - core) * half, 16), half)
@@ -393,7 +399,16 @@
     for k in range(1, nb):
         o = lax.rem(me + k, nb)
         go(copy_to(stage.at[o], spread.at[me], ps.at[k], pr.at[k], "brick", o))
-        go(copy_to(rec.at[o], arrived.at[me], rs.at[k], rr.at[k], "brick", o))
+    order = (3, 1, 0, 2)
+
+    def plane_of(x):
+        return pl.ds(x * PLANE, PLANE)
+
+    for x in order:
+        for k in range(1, nb):
+            o = lax.rem(me + k, nb)
+            go(copy_to(rec.at[o, :, plane_of(x)], arrived.at[me, :, plane_of(x)],
+                       rs.at[x, k], rr.at[x, k], "brick", o))
     band[...] = jnp.zeros_like(band)
     slopes[...] = jnp.zeros_like(slopes)
     terms[...] = jnp.zeros_like(terms)
@@ -409,29 +424,12 @@
     r_id = lax.broadcasted_iota(jnp.int32, (rows, rows), 0)
     c_id = lax.broadcasted_iota(jnp.int32, (rows, rows), 1)
     turn = jnp.where(r_id == home(c_id), 1.0, 0.0).astype(bf16)
+    local[2].wait()
     lined_cot = jnp.concatenate(
         [cot[:, :, z * pair:(z + 1) * pair].reshape(strip, pair) for z in range(BZ)], axis=0)
     turned = jnp.dot(turn, lined_cot, preferred_element_type=f32)
     cots[0] = turned[:, :C_OUT]
     cots[1] = turned[:, C_OUT:]
-    for k in range(1, nd):
-        s = lax.rem(dp + nd - k, nd)
-        copy_to(wt.at[mine], wts.at[s, mine], ws.at[k], wr.at[k], "dp", s).wait_recv()
-        go(copy_to(wts.at[s, mine], wts.at[s, mine], xs.at[k], xr.at[k], "brick", sib))
-    for k in range(1, nd):
-        s = lax.rem(dp + nd - k, nd)
-        copy_to(wt.at[theirs], wts.at[s, theirs], xs.at[k], xr.at[k], "brick", sib).wait_recv()
-    local[1].wait()
-    spots = {0: ((KB - C_IN, 0), (C_IN, NB)), 1: ((0, 0), (2 * C_IN, NB)), 2: ((C_IN, 0), (3 * C_IN, NB))}
-    for d in range(nd):
-        w = wts[d].astype(f32).T.astype(bf16)
-        for t in range(TAPS):
-            ab, e = divmod(t, 3)
-            for d2, r, take, off in row_parts(t * C_IN, C_IN, shard):
-                if d2 == d:
-                    for row, col in spots[e]:
-                        at = ab * KB + row + off
-                        band[at:at + take, col:col + C_OUT] = w[r:r + take]
     sy = shift_matrix(n, 1, 0)
     sz = shift_matrix(n, 0, 1)
     syz = shift_matrix(n, 1, 1)
@@ -439,9 +437,6 @@
         s = lax.rem(me + nb - k, nb)
         copy_to(stage.at[s], spread.at[s], ps.at[k], pr.at[k], "brick", s).wait_recv()
     spread[me] = stage[me]
-    for k in range(1, nb):
-        s = lax.rem(me + nb - k, nb)
-        copy_to(rec.at[s], arrived.at[s], rs.at[k], rr.at[k], "brick", s).wait_recv()
     local[0].wait()
     held = spread[0]
     for s in range(1, nb):
@@ -451,15 +446,15 @@
 
     def place_plane(x):
         lanes = slice(x * PLANE, (x + 1) * PLANE)
+        for k in range(1, nb):
+            s = lax.rem(me + nb - k, nb)
+            copy_to(rec.at[s, :, plane_of(x)], arrived.at[s, :, plane_of(x)],
+                    rs.at[x, k], rr.at[x, k], "brick", s).wait_recv()
         records = arrived[:, :, lanes].reshape(nb * cap, PLANE)
         filled[:, lanes] = jnp.dot(pick, records, preferred_element_type=f32).astype(bf16)
 
     last = slice((BS - 1) * PLANE, BS * PLANE)
-    place_plane(BS - 1)
     edge = copy_to(filled.at[n - n // BX:n, last], rim, bs, br, "brick", lax.rem(me + 1, nb))
-    pl.when(me < nb - 1)(edge.start)
-    for x in range(BS - 1):
-        place_plane(x)
 
     def move(s, v):
         return jnp.dot(s, v, preferred_element_type=f32).astype(bf16)
@@ -483,18 +478,52 @@
                         cols[q, k:k + ROW] = whole
                         cols[q, k + ROW:k + KB] = tail
 
-    def forward(ox):
+    def forward(ox, a, first=False):
+        q = slice(ox * 2 * n, (ox + 1) * 2 * n)
+        k = slice(a * 3 * KB, (a + 1) * 3 * KB)
+        part = jnp.dot(cols[q, k], band[k, :], preferred_element_type=f32)
+        linear[q, :] = part if first else linear[q, :] + part
+
+    def activate(ox):
         q = slice(ox * 2 * n, (ox + 1) * 2 * n)
         for oz in range(2):
-            v = jnp.dot(cols[q, :], band[:, oz * NB:(oz + 1) * NB], preferred_element_type=f32)[:, :C_OUT]
+            v = linear[q, oz * NB:oz * NB + C_OUT]
             s = 1.0 / (1.0 + jnp.exp(-v))
             acts[q, oz * C_OUT:(oz + 1) * C_OUT] = v * s
             slope = s * (1.0 + v * (1.0 - s))
             slopes[q, oz * NB:oz * NB + C_OUT] = (cots[oz, q, :] * slope).astype(bf16)
 
-    for x in range(BS):
+    def take_plane(x):
+        place_plane(x)
+        if x == BS - 1:
+            pl.when(me < nb - 1)(edge.start)
         fill_columns(x, filled[:, x * PLANE:(x + 1) * PLANE])
-    forward(1)
+
+    take_plane(3)
+    take_plane(1)
+    for k in range(1, nd):
+        s = lax.rem(dp + nd - k, nd)
+        copy_to(wt.at[mine], wts.at[s, mine], ws.at[k], wr.at[k], "dp", s).wait_recv()
+        go(copy_to(wts.at[s, mine], wts.at[s, mine], xs.at[k], xr.at[k], "brick", sib))
+    for k in range(1, nd):
+        s = lax.rem(dp + nd - k, nd)
+        copy_to(wt.at[theirs], wts.at[s, theirs], xs.at[k], xr.at[k], "brick", sib).wait_recv()
+    local[1].wait()
+    spots = {0: ((KB - C_IN, 0), (C_IN, NB)), 1: ((0, 0), (2 * C_IN, NB)), 2: ((C_IN, 0), (3 * C_IN, NB))}
+    for d in range(nd):
+        w = wts[d].astype(f32).T.astype(bf16)
+        for t in range(TAPS):
+            ab, e = divmod(t, 3)
+            for d2, r, take, off in row_parts(t * C_IN, C_IN, shard):
+                if d2 == d:
+                    for row, col in spots[e]:
+                        at = ab * KB + row + off
+                        band[at:at + take, col:col + C_OUT] = w[r:r + take]
+    forward(1, 2, True)
+    forward(0, 2, True)
+    forward(1, 0)
+    take_plane(0)
+    forward(0, 1)
 
     @pl.when(me > 0)
     def _():
@@ -505,7 +534,11 @@
         rim[...] = jnp.zeros_like(rim)
 
     fill_columns(-1, jnp.concatenate([rim[...], filled[:n - n // BX, last]], axis=0))
-    forward(0)
+    forward(0, 0)
+    activate(0)
+    take_plane(2)
+    forward(1, 1)
+    activate(1)
 
     def tap_rows(ab):
         g = lax.dot_general(cols[:, ab * KB:(ab + 1) * KB], slopes[...], (((0,), (0,)), ((), ())),
@@ -559,6 +592,8 @@
     for z in range(BZ):
         act_out[:, :, z * pair:(z + 1) * pair] = (
             shown[z * strip:(z + 1) * strip].astype(bf16).reshape(2 * BX, 2 * BY, pair))
+    stored = pltpu.make_async_copy(act_out, act_hbm, loc.at[5])
+    stored.start()
     for d in range(nd):
         to_rank(d)
     total = own[...]
@@ -587,6 +622,7 @@
             if take > 0:
                 grad[first + j * piece:first + j * piece + take, :] = final[j, :take, at:at + C_OUT]
     grad_out[...] = grad[...].T
+    stored.wait()
     for c in sent:
         c.wait_send()
     pl.when(me < nb - 1)(edge.wait_send)
@@ -613,13 +649,14 @@
             jax.ShapeDtypeStruct(cotangent.shape[1:], bf16),
             jax.ShapeDtypeStruct((C_OUT, shard), f32),
         ),
-        in_specs=[
-            pl.BlockSpec(memory_space=pl.ANY),
-            pl.BlockSpec(memory_space=pltpu.VMEM),
-            pl.BlockSpec(memory_space=pltpu.VMEM),
-            pl.BlockSpec(memory_space=pltpu.VMEM),
-        ],
+        in_specs=[pl.BlockSpec(memory_space=pl.ANY)] * 4,
+        out_specs=(pl.BlockSpec(memory_space=pl.ANY), pl.BlockSpec(memory_space=pltpu.VMEM)),
         scratch_shapes=[
+            vmem(cotangent.shape[1:], bf16),
+            vmem((nb, cap), jnp.int32),
+            vmem((C_OUT, shard), bf16),
+            vmem(cotangent.shape[1:], bf16),
+            vmem((4 * n, 2 * NB), f32),
             vmem((nb, 8, nb * cap), f32),
             vmem((nb, 8, nb * cap), f32),
             vmem(records.shape[1:], bf16),
@@ -640,13 +677,13 @@
             vmem((piece, wide), f32),
             vmem((nb, piece, wide), f32),
             vmem((shard, C_OUT), f32),
-            dma((nb,)), dma((nb,)), dma((nb,)), dma((nb,)),
-            dma((nd,)), dma((nd,)), dma((nd,)), dma((nd,)), dma((2,)), dma, dma,
+            dma((BS, nb)), dma((BS, nb)), dma((nb,)), dma((nb,)),
+            dma((nd,)), dma((nd,)), dma((nd,)), dma((nd,)), dma((6,)), dma, dma,
             dma((nd,)), dma((nd,)), dma((nd, nc)), dma((nd, nc)),
             dma((nd,)), dma((nd,)), dma((nc,)), dma((nc,)), dma((nc,)), dma((nc,)),
         ],
         compiler_params=pltpu.CompilerParams(
-            collective_id=2, has_side_effects=True, vmem_limit_bytes=VMEM_LIMIT),
+            collective_id=2, has_side_effects=True, vmem_limit_bytes=FUSED_LIMIT),
         name="fused",
     )(records.reshape(records.shape[1:]), positions.reshape(nb, cap), weight.T,
       cotangent.reshape(cotangent.shape[1:]))

time: 56.7 us -> 54 us (0.952)
  local copies, waits for them, and re-layouts: 5.61 us -> 3.68 us
  Pallas kernels: 50.2 us -> 49.4 us
    unnamed x10 -> x2, local copies, waits for them, and re-layouts: 5.61 us -> 3.68 us
    pallas_call x1, Pallas kernels: 50.2 us -> 49.4 us  [fused(): pl.pallas_call(functools.partial(fused_kernel, nb, nd, cap, shard, cut, p...]
where the time goes in v3:
time: 54 us; the launch traced here: 53.7 us
  Pallas kernels  49.4 us (91%)
  local copies, waits for them, and re-layouts  3.68 us (7%)
  between operations  0.64 us (1%)
    pallas_call x1, Pallas kernels, fused(): pl.pallas_call(functools.partial(fused_kernel, nb, nd, cap, shard, cut, p...  49.4 us
    unnamed x2, local copies, waits for them, and re-layouts  3.68 us

profile of v3, /device:TPU:25, one launch (start us, length us, event | category | flops | bytes accessed | tf_op | source)
XLA Modules:
  0.0 53.7 jit_solution(5946523426772887125)
XLA Ops:
  0.6 49.4 %fused.1 = (bf16[4,16,3072]{2,1,0:T(8,128)(2,1)}, f32[192,648]{1,0:T(8,128)}) custom-call(bf16[8,16,6144]{2,1,0:T(8,128)(2,1)} %bitcast.6, s32[8,16]{1,0:T(8,128)} %bitcast.11, bf16[192,648]{1,0:T(8,128)(2,1)} %bitcast.10, bf16[4,16,3072]{2,1,0:T(8,128)(2,1)} %bitcast.9), custom_call_target="tpu_custom_call" | custom-call | tf_op jit(solution)/shard_map/fused/pallas_call | solution.py:646
  50.1 1.8 %copy.8 = bf16[1,4,16,3072]{3,2,1,0:T(8,128)(2,1)} copy(bf16[1,4,16,3072]{3,2,1,0:T(8,128)(2,1)} %bitcast.8) | data formatting | bytes 786432
  51.8 1.9 %copy.9 = f32[648,192]{0,1:T(8,128)} copy(f32[648,192]{0,1:T(8,128)} %bitcast.7) | data formatting | bytes 995328

commit v4 on v3

--- a/solution.py
+++ b/solution.py
@@ -17,6 +17,7 @@
 PLANE = BS * BS * C_IN
 ROW = BS * C_IN
 KB = 512
+SIDE = 64
 NB = 256
 MESH = pl.DeviceIdType.MESH
 VMEM_LIMIT = 48 * 1024 * 1024
@@ -349,9 +350,9 @@
     return act.reshape(cotangent.shape), sum_terms(terms, nb, nd, shard, cut, piece)
 
 
-def fused_kernel(nb, nd, cap, shard, cut, piece, rec, pos_in, wt_in, cot_in, act_hbm, grad_out,
-                 act_out, pos, wt, cot, linear, stage, spread, arrived, wts, filled, rim, cols, band, slopes, cots, acts,
-                 terms, got, pass_on, plane_in, down, down_in, own, final, grad,
+def fused_kernel(nb, nd, cap, shard, main, piece, rec, pos_in, wt_in, cot_in, act_hbm, grad_out,
+                 act_out, pos, wt, cot, linear, stage, spread, arrived, wts, turned_wts, filled, rim, cols, band, slopes, cots, acts,
+                 terms, got, pass_on, plane_in, down, down_in, own, final,
                  rs, rr, ps, pr, ws, wr, xs, xr, loc, bs, br, s1, r1, s2, r2, s3, r3, s4, r4, s5, r5):
     f32, bf16 = jnp.float32, jnp.bfloat16
     n = BX * BY * BZ
@@ -499,19 +500,24 @@
             pl.when(me < nb - 1)(edge.start)
         fill_columns(x, filled[:, x * PLANE:(x + 1) * PLANE])
 
+    def turn_weights(d):
+        turned_wts[d] = wts[d].astype(f32).T.astype(bf16)
+
     take_plane(3)
     take_plane(1)
     for k in range(1, nd):
         s = lax.rem(dp + nd - k, nd)
         copy_to(wt.at[mine], wts.at[s, mine], ws.at[k], wr.at[k], "dp", s).wait_recv()
         go(copy_to(wts.at[s, mine], wts.at[s, mine], xs.at[k], xr.at[k], "brick", sib))
+    local[1].wait()
+    turn_weights(dp)
     for k in range(1, nd):
         s = lax.rem(dp + nd - k, nd)
         copy_to(wt.at[theirs], wts.at[s, theirs], xs.at[k], xr.at[k], "brick", sib).wait_recv()
-    local[1].wait()
+        turn_weights(s)
     spots = {0: ((KB - C_IN, 0), (C_IN, NB)), 1: ((0, 0), (2 * C_IN, NB)), 2: ((C_IN, 0), (3 * C_IN, NB))}
     for d in range(nd):
-        w = wts[d].astype(f32).T.astype(bf16)
+        w = turned_wts[d]
         for t in range(TAPS):
             ab, e = divmod(t, 3)
             for d2, r, take, off in row_parts(t * C_IN, C_IN, shard):
@@ -540,18 +546,28 @@
     forward(1, 1)
     activate(1)
 
-    def tap_rows(ab):
+    def put(d, r, rows, first):
+        count = rows.shape[0]
+        head = max(0, min(count, main - r))
+        spans = [(0, head, r, 0, 0, C_OUT)] if head else []
+        if head < count:
+            for m in range(C_OUT // SIDE):
+                spans.append((head, count, r + head - main + m * (shard - main), C_OUT, m * SIDE, SIDE))
+        for lo, hi, base, at, col, width in spans:
+            for j, row, tk, off in row_parts(base, hi - lo, piece):
+                part = rows[lo + off:lo + off + tk, col:col + width]
+                if not first:
+                    part = part + terms[d, j, row:row + tk, at:at + width]
+                terms[d, j, row:row + tk, at:at + width] = part
+
+    def tap_rows(ab, first=True):
         g = lax.dot_general(cols[:, ab * KB:(ab + 1) * KB], slopes[...], (((0,), (0,)), ((), ())),
                             preferred_element_type=f32)
         for e in range(3):
             (r0, c0), (r1, c1) = spots[e]
             tap = g[r0:r0 + C_IN, c0:c0 + C_OUT] + g[r1:r1 + C_IN, c1:c1 + C_OUT]
             for d, r, take, off in row_parts((ab * 3 + e) * C_IN, C_IN, shard):
-                left = max(0, min(take, cut - r))
-                for start, length, base, at in ((off, left, r, 0), (off + left, take - left, r + left - cut, C_OUT)):
-                    if length:
-                        for j, row, tk, o2 in row_parts(base, length, piece):
-                            terms[d, j, row:row + tk, at:at + C_OUT] = tap[start + o2:start + o2 + tk]
+                put(d, r, tap[off:off + take], first)
 
     def to_sibling(d):
         return copy_to(terms.at[d, pl.ds((1 - core) * nc, nc)], got.at[d], s1.at[d], r1.at[d], "brick", sib)
@@ -591,7 +607,7 @@
     shown = lax.dot_general(turn, acts[...].astype(bf16), (((0,), (0,)), ((), ())), preferred_element_type=f32)
     for z in range(BZ):
         act_out[:, :, z * pair:(z + 1) * pair] = (
-            shown[z * strip:(z + 1) * strip].astype(bf16).reshape(2 * BX, 2 * BY, pair))
+            shown[z * strip:(z + 1) * strip].reshape(2 * BX, 2 * BY, pair))
     stored = pltpu.make_async_copy(act_out, act_hbm, loc.at[5])
     stored.start()
     for d in range(nd):
@@ -617,11 +633,10 @@
         there = final.at[(1 - core) * nc + q]
         copy_to(there, there, s5.at[k], r5.at[k], "brick", sib).wait_recv()
     for j in range(nb):
-        for count, first, at in ((cut, 0, 0), (shard - cut, cut, C_OUT)):
-            take = min(piece, count - j * piece)
-            if take > 0:
-                grad[first + j * piece:first + j * piece + take, :] = final[j, :take, at:at + C_OUT]
-    grad_out[...] = grad[...].T
+        grad_out[j * piece:(j + 1) * piece, :] = final[j, :, :C_OUT]
+    for m in range(C_OUT // SIDE):
+        for j, row, tk, off in row_parts(m * (shard - main), shard - main, piece):
+            grad_out[main + off:main + off + tk, m * SIDE:(m + 1) * SIDE] = final[j, row:row + tk, C_OUT:]
     stored.wait()
     for c in sent:
         c.wait_send()
@@ -635,24 +650,24 @@
 def fused(nb, nd, records, positions, weight, cotangent):
     cap = records.shape[2]
     shard = weight.shape[0]
-    cut = up(-(-shard // 2), 8)
-    piece = up(-(-cut // nb), 16)
+    main = up(-(-shard * C_OUT // (C_OUT + SIDE)), nb * 16)
+    piece = main // nb
     f32, bf16 = jnp.float32, jnp.bfloat16
     n = BX * BY * BZ
     nc = nb // 2
-    wide = 2 * C_OUT
+    wide = C_OUT + SIDE
     dma = pltpu.SemaphoreType.DMA
     vmem = pltpu.VMEM
     act, grad = pl.pallas_call(
-        functools.partial(fused_kernel, nb, nd, cap, shard, cut, piece),
+        functools.partial(fused_kernel, nb, nd, cap, shard, main, piece),
         out_shape=(
-            jax.ShapeDtypeStruct(cotangent.shape[1:], bf16),
-            jax.ShapeDtypeStruct((C_OUT, shard), f32),
+            jax.ShapeDtypeStruct(cotangent.shape[1:], f32),
+            jax.ShapeDtypeStruct((shard, C_OUT), f32),
         ),
         in_specs=[pl.BlockSpec(memory_space=pl.ANY)] * 4,
         out_specs=(pl.BlockSpec(memory_space=pl.ANY), pl.BlockSpec(memory_space=pltpu.VMEM)),
         scratch_shapes=[
-            vmem(cotangent.shape[1:], bf16),
+            vmem(cotangent.shape[1:], f32),
             vmem((nb, cap), jnp.int32),
             vmem((C_OUT, shard), bf16),
             vmem(cotangent.shape[1:], bf16),
@@ -661,13 +676,14 @@
             vmem((nb, 8, nb * cap), f32),
             vmem(records.shape[1:], bf16),
             vmem((nd, C_OUT, shard), bf16),
+            vmem((nd, shard, C_OUT), bf16),
             vmem((n, BS * PLANE), bf16),
             vmem((n // BX, PLANE), bf16),
             vmem((4 * n, 9 * KB), bf16),
             vmem((9 * KB, 2 * NB), bf16),
             vmem((4 * n, 2 * NB), bf16),
             vmem((2, 4 * n, C_OUT), f32),
-            vmem((4 * n, wide), f32),
+            vmem((4 * n, 2 * C_OUT), f32),
             vmem((nd, nb, piece, wide), f32),
             vmem((nd, nc, piece, wide), f32),
             vmem((nd, nc, piece, wide), bf16),
@@ -676,7 +692,6 @@
             vmem((nd, piece, wide), bf16),
             vmem((piece, wide), f32),
             vmem((nb, piece, wide), f32),
-            vmem((shard, C_OUT), f32),
             dma((BS, nb)), dma((BS, nb)), dma((nb,)), dma((nb,)),
             dma((nd,)), dma((nd,)), dma((nd,)), dma((nd,)), dma((6,)), dma, dma,
             dma((nd,)), dma((nd,)), dma((nd, nc)), dma((nd, nc)),
@@ -687,7 +702,7 @@
         name="fused",
     )(records.reshape(records.shape[1:]), positions.reshape(nb, cap), weight.T,
       cotangent.reshape(cotangent.shape[1:]))
-    return act.reshape(cotangent.shape), grad.T
+    return act.astype(bf16).reshape(cotangent.shape), grad
 
 
 def body(nb, nd, records, positions, weight, cotangent):

time: 54 us -> 51.9 us (0.961)
  local copies, waits for them, and re-layouts: 3.68 us -> 1.07 us
  other arithmetic: 0 us -> 1.98 us
  Pallas kernels: 49.4 us -> 48 us
    unnamed x2 -> x3, local copies, waits for them, and re-layouts: 3.68 us -> 1.07 us
    reshape x0 -> x1, other arithmetic: none -> 1.98 us  [fused(): return (act.astype(bf16).reshape(cotangent.shape), grad)]
    pallas_call x1, Pallas kernels: 49.4 us -> 48 us  [fused(): pl.pallas_call(functools.partial(fused_kernel, nb, nd, cap, shard, main,...]
where the time goes in v4:
time: 51.9 us; the launch traced here: 51.7 us
  Pallas kernels  48 us (92%)
  other arithmetic  1.98 us (4%)
  local copies, waits for them, and re-layouts  1.07 us (2%)
  between operations  0.65 us (1%)
    pallas_call x1, Pallas kernels, fused(): pl.pallas_call(functools.partial(fused_kernel, nb, nd, cap, shard, main,...  48 us
    reshape x1, other arithmetic, fused(): return (act.astype(bf16).reshape(cotangent.shape), grad)  1.98 us
    unnamed x3, local copies, waits for them, and re-layouts  1.07 us

profile of v4, /device:TPU:25, one launch (start us, length us, event | category | flops | bytes accessed | tf_op | source)
XLA Modules:
  0.0 51.7 jit_solution(7693868822367919005)
XLA Ops:
  0.6 48.0 %fused.1 = (f32[4,16,3072]{2,1,0:T(8,128)}, f32[648,192]{1,0:T(8,128)}) custom-call(bf16[8,16,6144]{2,1,0:T(8,128)(2,1)} %bitcast.6, s32[8,16]{1,0:T(8,128)} %bitcast.9, bf16[192,648]{1,0:T(8,128)(2,1)} %bitcast.8, bf16[4,16,3072]{2,1,0:T(8,128)(2,1)} %bitcast.7), custom_call_target="tpu_custom_call" | custom-call | tf_op jit(solution)/shard_map/fused/pallas_call | solution.py:661
  48.6 0.0 copy-start
  48.6 2.0 %convert_bitcast_fusion = bf16[1,4,16,3072]{3,2,1,0:T(8,128)(2,1)} fusion(f32[4,16,3072]{2,1,0:T(8,128)} %get-tuple-element.4), kind=kLoop, calls=%fused_computation | loop fusion | flops 196608 | bytes 1179648 | tf_op jit(solution)/shard_map/reshape | solution.py:705
  50.6 0.0 copy-done
  50.6 1.1 %copy.6 = f32[648,192]{0,1:T(8,128)} copy(f32[648,192]{1,0:T(8,128)S(1)} %copy-done) | data formatting | bytes 995328
Async XLA Ops:
  48.6 2.0 %copy-start = (f32[648,192]{1,0:T(8,128)S(1)}, f32[648,192]{1,0:T(8,128)}, u32[]{:S(2)}) copy-start(f32[648,192]{1,0:T(8,128)} %get-tuple-element.7) | copy-start | bytes 1492996

commit v5 on v4

--- a/solution.py
+++ b/solution.py
@@ -503,12 +503,11 @@
     def turn_weights(d):
         turned_wts[d] = wts[d].astype(f32).T.astype(bf16)
 
-    take_plane(3)
-    take_plane(1)
     for k in range(1, nd):
         s = lax.rem(dp + nd - k, nd)
         copy_to(wt.at[mine], wts.at[s, mine], ws.at[k], wr.at[k], "dp", s).wait_recv()
         go(copy_to(wts.at[s, mine], wts.at[s, mine], xs.at[k], xr.at[k], "brick", sib))
+    take_plane(3)
     local[1].wait()
     turn_weights(dp)
     for k in range(1, nd):
@@ -525,6 +524,7 @@
                     for row, col in spots[e]:
                         at = ab * KB + row + off
                         band[at:at + take, col:col + C_OUT] = w[r:r + take]
+    take_plane(1)
     forward(1, 2, True)
     forward(0, 2, True)
     forward(1, 0)
@@ -542,10 +542,6 @@
     fill_columns(-1, jnp.concatenate([rim[...], filled[:n - n // BX, last]], axis=0))
     forward(0, 0)
     activate(0)
-    take_plane(2)
-    forward(1, 1)
-    activate(1)
-
     def put(d, r, rows, first):
         count = rows.shape[0]
         head = max(0, min(count, main - r))
@@ -560,8 +556,9 @@
                     part = part + terms[d, j, row:row + tk, at:at + width]
                 terms[d, j, row:row + tk, at:at + width] = part
 
-    def tap_rows(ab, first=True):
-        g = lax.dot_general(cols[:, ab * KB:(ab + 1) * KB], slopes[...], (((0,), (0,)), ((), ())),
+    def tap_rows(ab, ox, first):
+        q = slice(ox * 2 * n, (ox + 1) * 2 * n)
+        g = lax.dot_general(cols[q, ab * KB:(ab + 1) * KB], slopes[q, :], (((0,), (0,)), ((), ())),
                             preferred_element_type=f32)
         for e in range(3):
             (r0, c0), (r1, c1) = spots[e]
@@ -569,6 +566,12 @@
             for d, r, take, off in row_parts((ab * 3 + e) * C_IN, C_IN, shard):
                 put(d, r, tap[off:off + take], first)
 
+    for ab in range(9):
+        tap_rows(ab, 0, True)
+    take_plane(2)
+    forward(1, 1)
+    activate(1)
+
     def to_sibling(d):
         return copy_to(terms.at[d, pl.ds((1 - core) * nc, nc)], got.at[d], s1.at[d], r1.at[d], "brick", sib)
 
@@ -579,6 +582,16 @@
             pass_on[d, k] = (terms[d, core * nc + q] + got[d, q]).astype(bf16)
             go(copy_to(pass_on.at[d, k], plane_in.at[d, k], s2.at[d, k], r2.at[d, k], "brick", q * 2 + core))
 
+    half_rows = [pl.ds(h * (piece // 2), piece // 2) for h in range(2)]
+
+    def to_dp(d, h, peer):
+        return copy_to(down.at[d, half_rows[h]], down_in.at[dp, half_rows[h]], s3.at[d, h], r3.at[dp, h], "dp", peer)
+
+    def from_dp(k, h):
+        s = lax.rem(dp + nd - k, nd)
+        copy_to(down.at[s, half_rows[h]], down_in.at[s, half_rows[h]], s3.at[s, h], r3.at[s, h], "dp", s).wait_recv()
+        return down_in[s, half_rows[h], :].astype(f32)
+
     def to_rank(d):
         total = terms[d, core * nc + chip] + got[d, chip]
         for k in range(1, nc):
@@ -593,11 +606,12 @@
         @pl.when(dp != d)
         def _():
             down[d] = total.astype(bf16)
-            copy_to(down.at[d], down_in.at[dp], s3.at[d], r3.at[dp], "dp", d).start()
+            for h in range(2):
+                to_dp(d, h, d).start()
 
     ready = 0
     for ab in range(9):
-        tap_rows(ab)
+        tap_rows(ab, 1, False)
         while ready < nd and (ready + 1) * shard <= (ab + 1) * 3 * C_IN:
             go(to_sibling(ready))
             if ready:
@@ -612,26 +626,29 @@
     stored.start()
     for d in range(nd):
         to_rank(d)
-    total = own[...]
-    for k in range(1, nd):
-        s = lax.rem(dp + nd - k, nd)
-        copy_to(down.at[s], down_in.at[s], s3.at[s], r3.at[s], "dp", s).wait_recv()
-        total = total + down_in[s].astype(f32)
     here = core * nc + chip
-    final[here] = total
-    for k in range(1, nc):
-        q = lax.rem(chip + k, nc)
-        go(copy_to(final.at[here], final.at[here], s4.at[k], r4.at[k], "brick", q * 2 + core))
-    go(copy_to(final.at[here], final.at[here], s5.at[0], r5.at[0], "brick", sib))
-    for k in range(1, nc):
-        q = lax.rem(chip + nc - k, nc)
-        there = final.at[core * nc + q]
-        copy_to(there, there, s4.at[k], r4.at[k], "brick", q * 2 + core).wait_recv()
-        go(copy_to(there, there, s5.at[k], r5.at[k], "brick", sib))
-    for k in range(nc):
-        q = lax.rem(chip + nc - k, nc)
-        there = final.at[(1 - core) * nc + q]
-        copy_to(there, there, s5.at[k], r5.at[k], "brick", sib).wait_recv()
+    for h in range(2):
+        part = half_rows[h]
+        total = own[part, :]
+        for k in range(1, nd):
+            total = total + from_dp(k, h)
+        final[here, part, :] = total
+        slot = final.at[here, part]
+        for k in range(1, nc):
+            q = lax.rem(chip + k, nc)
+            go(copy_to(slot, slot, s4.at[h, k], r4.at[h, k], "brick", q * 2 + core))
+        go(copy_to(slot, slot, s5.at[h, 0], r5.at[h, 0], "brick", sib))
+    for h in range(2):
+        for k in range(1, nc):
+            q = lax.rem(chip + nc - k, nc)
+            there = final.at[core * nc + q, half_rows[h]]
+            copy_to(there, there, s4.at[h, k], r4.at[h, k], "brick", q * 2 + core).wait_recv()
+            go(copy_to(there, there, s5.at[h, k], r5.at[h, k], "brick", sib))
+    for h in range(2):
+        for k in range(nc):
+            q = lax.rem(chip + nc - k, nc)
+            there = final.at[(1 - core) * nc + q, half_rows[h]]
+            copy_to(there, there, s5.at[h, k], r5.at[h, k], "brick", sib).wait_recv()
     for j in range(nb):
         grad_out[j * piece:(j + 1) * piece, :] = final[j, :, :C_OUT]
     for m in range(C_OUT // SIDE):
@@ -644,7 +661,8 @@
     for d in range(nd):
         @pl.when(dp != d)
         def _():
-            copy_to(down.at[d], down_in.at[dp], s3.at[d], r3.at[dp], "dp", d).wait_send()
+            for h in range(2):
+                to_dp(d, h, d).wait_send()
 
 
 def fused(nb, nd, records, positions, weight, cotangent):
@@ -695,7 +713,7 @@
             dma((BS, nb)), dma((BS, nb)), dma((nb,)), dma((nb,)),
             dma((nd,)), dma((nd,)), dma((nd,)), dma((nd,)), dma((6,)), dma, dma,
             dma((nd,)), dma((nd,)), dma((nd, nc)), dma((nd, nc)),
-            dma((nd,)), dma((nd,)), dma((nc,)), dma((nc,)), dma((nc,)), dma((nc,)),
+            dma((nd, 2)), dma((nd, 2)), dma((2, nc)), dma((2, nc)), dma((2, nc)), dma((2, nc)),
         ],
         compiler_params=pltpu.CompilerParams(
             collective_id=2, has_side_effects=True, vmem_limit_bytes=FUSED_LIMIT),

time: 51.9 us -> 52.8 us (1.017)
  Pallas kernels: 48 us -> 48.9 us
    pallas_call x1, Pallas kernels: 48 us -> 48.9 us  [fused(): pl.pallas_call(functools.partial(fused_kernel, nb, nd, cap, shard, main,...]
where the time goes in v5:
time: 52.8 us; the launch traced here: 52.6 us
  Pallas kernels  48.9 us (93%)
  other arithmetic  1.98 us (4%)
  local copies, waits for them, and re-layouts  1.07 us (2%)
  between operations  0.65 us (1%)
    pallas_call x1, Pallas kernels, fused(): pl.pallas_call(functools.partial(fused_kernel, nb, nd, cap, shard, main,...  48.9 us
    reshape x1, other arithmetic, fused(): return (act.astype(bf16).reshape(cotangent.shape), grad)  1.98 us
    unnamed x3, local copies, waits for them, and re-layouts  1.07 us

profile of v5, /device:TPU:25, one launch (start us, length us, event | category | flops | bytes accessed | tf_op | source)
XLA Modules:
  0.0 52.6 jit_solution(6944386669999979572)
XLA Ops:
  0.6 48.9 %fused.1 = (f32[4,16,3072]{2,1,0:T(8,128)}, f32[648,192]{1,0:T(8,128)}) custom-call(bf16[8,16,6144]{2,1,0:T(8,128)(2,1)} %bitcast.6, s32[8,16]{1,0:T(8,128)} %bitcast.9, bf16[192,648]{1,0:T(8,128)(2,1)} %bitcast.8, bf16[4,16,3072]{2,1,0:T(8,128)(2,1)} %bitcast.7), custom_call_target="tpu_custom_call" | custom-call | tf_op jit(solution)/shard_map/fused/pallas_call | solution.py:679
  49.5 0.0 copy-start
  49.5 2.0 %convert_bitcast_fusion = bf16[1,4,16,3072]{3,2,1,0:T(8,128)(2,1)} fusion(f32[4,16,3072]{2,1,0:T(8,128)} %get-tuple-element.4), kind=kLoop, calls=%fused_computation | loop fusion | flops 196608 | bytes 1179648 | tf_op jit(solution)/shard_map/reshape | solution.py:723
  51.5 0.0 copy-done
  51.5 1.1 %copy.6 = f32[648,192]{0,1:T(8,128)} copy(f32[648,192]{1,0:T(8,128)S(1)} %copy-done) | data formatting | bytes 995328
Async XLA Ops:
  49.5 2.0 %copy-start = (f32[648,192]{1,0:T(8,128)S(1)}, f32[648,192]{1,0:T(8,128)}, u32[]{:S(2)}) copy-start(f32[648,192]{1,0:T(8,128)} %get-tuple-element.7) | copy-start | bytes 1492996

commit v6 on v5

--- a/solution.py
+++ b/solution.py
@@ -351,9 +351,9 @@
 
 
 def fused_kernel(nb, nd, cap, shard, main, piece, rec, pos_in, wt_in, cot_in, act_hbm, grad_out,
-                 act_out, pos, wt, cot, linear, stage, spread, arrived, wts, turned_wts, filled, rim, cols, band, slopes, cots, acts,
+                 act_out, pos, wt, cot, linear, stage, spread, arrived, wts, tails, turned_wts, filled, rim, cols, band, slopes, cots, acts,
                  terms, got, pass_on, plane_in, down, down_in, own, final,
-                 rs, rr, ps, pr, ws, wr, xs, xr, loc, bs, br, s1, r1, s2, r2, s3, r3, s4, r4, s5, r5):
+                 rs, rr, ps, pr, ws, wr, ts, tr, xs, xr, loc, bs, br, s1, r1, s2, r2, s3, r3, s4, r4, s5, r5):
     f32, bf16 = jnp.float32, jnp.bfloat16
     n = BX * BY * BZ
     nc = nb // 2
@@ -386,8 +386,12 @@
     pl.semaphore_wait(barrier, nb + nd - 2)
     local[3].wait()
     half = wt.shape[0] // 2
-    mine = pl.ds(pl.multiple_of(core * half, 16), half)
-    theirs = pl.ds(pl.multiple_of((1 - core) * half, 16), half)
+    body_lanes = shard - shard % 128
+    mine = (pl.ds(pl.multiple_of(core * half, 16), half), pl.ds(0, body_lanes))
+    theirs = (pl.ds(pl.multiple_of((1 - core) * half, 16), half), pl.ds(0, body_lanes))
+    tail_rows = shard - body_lanes
+    if tail_rows:
+        tails[dp, :tail_rows, :] = wt[:, body_lanes:].astype(f32).T
     sent = []
 
     def go(c):
@@ -396,7 +400,9 @@
 
     for k in range(1, nd):
         o = lax.rem(dp + k, nd)
-        go(copy_to(wt.at[mine], wts.at[dp, mine], ws.at[k], wr.at[k], "dp", o))
+        go(copy_to(wt.at[mine], wts.at[(dp,) + mine], ws.at[k], wr.at[k], "dp", o))
+        if tail_rows:
+            go(copy_to(tails.at[dp], tails.at[dp], ts.at[k], tr.at[k], "dp", o))
     for k in range(1, nb):
         o = lax.rem(me + k, nb)
         go(copy_to(stage.at[o], spread.at[me], ps.at[k], pr.at[k], "brick", o))
@@ -501,18 +507,22 @@
         fill_columns(x, filled[:, x * PLANE:(x + 1) * PLANE])
 
     def turn_weights(d):
-        turned_wts[d] = wts[d].astype(f32).T.astype(bf16)
-
+        turned_wts[d, :body_lanes, :] = wts[d, :, :body_lanes].astype(f32).T.astype(bf16)
+        if tail_rows:
+            turned_wts[d, body_lanes:, :] = tails[d, :tail_rows, :].astype(bf16)
+
+    take_plane(3)
     for k in range(1, nd):
         s = lax.rem(dp + nd - k, nd)
-        copy_to(wt.at[mine], wts.at[s, mine], ws.at[k], wr.at[k], "dp", s).wait_recv()
-        go(copy_to(wts.at[s, mine], wts.at[s, mine], xs.at[k], xr.at[k], "brick", sib))
-    take_plane(3)
+        copy_to(wt.at[mine], wts.at[(s,) + mine], ws.at[k], wr.at[k], "dp", s).wait_recv()
+        go(copy_to(wts.at[(s,) + mine], wts.at[(s,) + mine], xs.at[k], xr.at[k], "brick", sib))
     local[1].wait()
     turn_weights(dp)
     for k in range(1, nd):
         s = lax.rem(dp + nd - k, nd)
-        copy_to(wt.at[theirs], wts.at[s, theirs], xs.at[k], xr.at[k], "brick", sib).wait_recv()
+        copy_to(wt.at[theirs], wts.at[(s,) + theirs], xs.at[k], xr.at[k], "brick", sib).wait_recv()
+        if tail_rows:
+            copy_to(tails.at[s], tails.at[s], ts.at[k], tr.at[k], "dp", s).wait_recv()
         turn_weights(s)
     spots = {0: ((KB - C_IN, 0), (C_IN, NB)), 1: ((0, 0), (2 * C_IN, NB)), 2: ((C_IN, 0), (3 * C_IN, NB))}
     for d in range(nd):
@@ -542,7 +552,7 @@
     fill_columns(-1, jnp.concatenate([rim[...], filled[:n - n // BX, last]], axis=0))
     forward(0, 0)
     activate(0)
-    def put(d, r, rows, first):
+    def put(d, r, rows):
         count = rows.shape[0]
         head = max(0, min(count, main - r))
         spans = [(0, head, r, 0, 0, C_OUT)] if head else []
@@ -552,22 +562,17 @@
         for lo, hi, base, at, col, width in spans:
             for j, row, tk, off in row_parts(base, hi - lo, piece):
                 part = rows[lo + off:lo + off + tk, col:col + width]
-                if not first:
-                    part = part + terms[d, j, row:row + tk, at:at + width]
                 terms[d, j, row:row + tk, at:at + width] = part
 
-    def tap_rows(ab, ox, first):
-        q = slice(ox * 2 * n, (ox + 1) * 2 * n)
-        g = lax.dot_general(cols[q, ab * KB:(ab + 1) * KB], slopes[q, :], (((0,), (0,)), ((), ())),
+    def tap_rows(ab):
+        g = lax.dot_general(cols[:, ab * KB:(ab + 1) * KB], slopes[...], (((0,), (0,)), ((), ())),
                             preferred_element_type=f32)
         for e in range(3):
             (r0, c0), (r1, c1) = spots[e]
             tap = g[r0:r0 + C_IN, c0:c0 + C_OUT] + g[r1:r1 + C_IN, c1:c1 + C_OUT]
             for d, r, take, off in row_parts((ab * 3 + e) * C_IN, C_IN, shard):
-                put(d, r, tap[off:off + take], first)
-
-    for ab in range(9):
-        tap_rows(ab, 0, True)
+                put(d, r, tap[off:off + take])
+
     take_plane(2)
     forward(1, 1)
     activate(1)
@@ -611,7 +616,7 @@
 
     ready = 0
     for ab in range(9):
-        tap_rows(ab, 1, False)
+        tap_rows(ab)
         while ready < nd and (ready + 1) * shard <= (ab + 1) * 3 * C_IN:
             go(to_sibling(ready))
             if ready:
@@ -694,6 +699,7 @@
             vmem((nb, 8, nb * cap), f32),
             vmem(records.shape[1:], bf16),
             vmem((nd, C_OUT, shard), bf16),
+            vmem((nd, up(max(shard % 128, 1), 8), C_OUT), f32),
             vmem((nd, shard, C_OUT), bf16),
             vmem((n, BS * PLANE), bf16),
             vmem((n // BX, PLANE), bf16),
@@ -711,7 +717,7 @@
             vmem((piece, wide), f32),
             vmem((nb, piece, wide), f32),
             dma((BS, nb)), dma((BS, nb)), dma((nb,)), dma((nb,)),
-            dma((nd,)), dma((nd,)), dma((nd,)), dma((nd,)), dma((6,)), dma, dma,
+            dma((nd,)), dma((nd,)), dma((nd,)), dma((nd,)), dma((nd,)), dma((nd,)), dma((6,)), dma, dma,
             dma((nd,)), dma((nd,)), dma((nd, nc)), dma((nd, nc)),
             dma((nd, 2)), dma((nd, 2)), dma((2, nc)), dma((2, nc)), dma((2, nc)), dma((2, nc)),
         ],

time: 52.8 us -> 51.9 us (0.983)
  Pallas kernels: 48.9 us -> 48 us
    pallas_call x1, Pallas kernels: 48.9 us -> 48 us  [fused(): pl.pallas_call(functools.partial(fused_kernel, nb, nd, cap, shard, main,...]
where the time goes in v6:
time: 51.9 us; the launch traced here: 51.7 us
  Pallas kernels  48 us (92%)
  other arithmetic  1.98 us (4%)
  local copies, waits for them, and re-layouts  1.07 us (2%)
  between operations  0.65 us (1%)
    pallas_call x1, Pallas kernels, fused(): pl.pallas_call(functools.partial(fused_kernel, nb, nd, cap, shard, main,...  48 us
    reshape x1, other arithmetic, fused(): return (act.astype(bf16).reshape(cotangent.shape), grad)  1.98 us
    unnamed x3, local copies, waits for them, and re-layouts  1.07 us

profile of v6, /device:TPU:25, one launch (start us, length us, event | category | flops | bytes accessed | tf_op | source)
XLA Modules:
  0.0 51.7 jit_solution(3208285024559691622)
XLA Ops:
  0.6 48.0 %fused.1 = (f32[4,16,3072]{2,1,0:T(8,128)}, f32[648,192]{1,0:T(8,128)}) custom-call(bf16[8,16,6144]{2,1,0:T(8,128)(2,1)} %bitcast.6, s32[8,16]{1,0:T(8,128)} %bitcast.9, bf16[192,648]{1,0:T(8,128)(2,1)} %bitcast.8, bf16[4,16,3072]{2,1,0:T(8,128)(2,1)} %bitcast.7), custom_call_target="tpu_custom_call" | custom-call | tf_op jit(solution)/shard_map/fused/pallas_call | solution.py:684
  48.6 0.0 copy-start
  48.7 2.0 %convert_bitcast_fusion = bf16[1,4,16,3072]{3,2,1,0:T(8,128)(2,1)} fusion(f32[4,16,3072]{2,1,0:T(8,128)} %get-tuple-element.4), kind=kLoop, calls=%fused_computation | loop fusion | flops 196608 | bytes 1179648 | tf_op jit(solution)/shard_map/reshape | solution.py:729
  50.6 0.0 copy-done
  50.6 1.1 %copy.6 = f32[648,192]{0,1:T(8,128)} copy(f32[648,192]{1,0:T(8,128)S(1)} %copy-done) | data formatting | bytes 995328
Async XLA Ops:
  48.6 2.0 %copy-start = (f32[648,192]{1,0:T(8,128)S(1)}, f32[648,192]{1,0:T(8,128)}, u32[]{:S(2)}) copy-start(f32[648,192]{1,0:T(8,128)} %get-tuple-element.7) | copy-start | bytes 1492996

commit v7 on v6

--- a/solution.py
+++ b/solution.py
@@ -376,6 +376,33 @@
     ]
     for c in reversed(local):
         c.start()
+    pl.semaphore_wait(barrier, nb + nd - 2)
+    half = wt.shape[0] // 2
+    body_lanes = shard - shard % 128
+    mine = (pl.ds(pl.multiple_of(core * half, 16), half), pl.ds(0, body_lanes))
+    theirs = (pl.ds(pl.multiple_of((1 - core) * half, 16), half), pl.ds(0, body_lanes))
+    tail_rows = shard - body_lanes
+    sent = []
+
+    def go(c):
+        c.start()
+        sent.append(c)
+
+    for k in range(1, nd):
+        o = lax.rem(dp + k, nd)
+        go(copy_to(wt_in.at[mine], wts.at[(dp,) + mine], ws.at[k], wr.at[k], "dp", o))
+    order = (3, 1, 0, 2)
+
+    def plane_of(x):
+        return pl.ds(x * PLANE, PLANE)
+
+    def send_plane(x):
+        for k in range(1, nb):
+            o = lax.rem(me + k, nb)
+            go(copy_to(rec.at[o, :, plane_of(x)], arrived.at[me, :, plane_of(x)],
+                       rs.at[x, k], rr.at[x, k], "brick", o))
+
+    send_plane(order[0])
     local[4].wait()
     lane = lax.broadcasted_iota(jnp.int32, (cap, nb * cap), 1)
     slot = lax.broadcasted_iota(jnp.int32, (cap, nb * cap), 0)
@@ -383,39 +410,16 @@
     lined = jnp.dot(pos[...].astype(f32).astype(bf16), to_lanes, preferred_element_type=f32)
     for o in range(nb):
         stage[o] = jnp.broadcast_to(lined[o:o + 1], stage.shape[1:])
-    pl.semaphore_wait(barrier, nb + nd - 2)
+    for k in range(1, nb):
+        o = lax.rem(me + k, nb)
+        go(copy_to(stage.at[o], spread.at[me], ps.at[k], pr.at[k], "brick", o))
+    for x in order[1:]:
+        send_plane(x)
     local[3].wait()
-    half = wt.shape[0] // 2
-    body_lanes = shard - shard % 128
-    mine = (pl.ds(pl.multiple_of(core * half, 16), half), pl.ds(0, body_lanes))
-    theirs = (pl.ds(pl.multiple_of((1 - core) * half, 16), half), pl.ds(0, body_lanes))
-    tail_rows = shard - body_lanes
     if tail_rows:
         tails[dp, :tail_rows, :] = wt[:, body_lanes:].astype(f32).T
-    sent = []
-
-    def go(c):
-        c.start()
-        sent.append(c)
-
-    for k in range(1, nd):
-        o = lax.rem(dp + k, nd)
-        go(copy_to(wt.at[mine], wts.at[(dp,) + mine], ws.at[k], wr.at[k], "dp", o))
-        if tail_rows:
-            go(copy_to(tails.at[dp], tails.at[dp], ts.at[k], tr.at[k], "dp", o))
-    for k in range(1, nb):
-        o = lax.rem(me + k, nb)
-        go(copy_to(stage.at[o], spread.at[me], ps.at[k], pr.at[k], "brick", o))
-    order = (3, 1, 0, 2)
-
-    def plane_of(x):
-        return pl.ds(x * PLANE, PLANE)
-
-    for x in order:
-        for k in range(1, nb):
-            o = lax.rem(me + k, nb)
-            go(copy_to(rec.at[o, :, plane_of(x)], arrived.at[me, :, plane_of(x)],
-                       rs.at[x, k], rr.at[x, k], "brick", o))
+        for k in range(1, nd):
+            go(copy_to(tails.at[dp], tails.at[dp], ts.at[k], tr.at[k], "dp", lax.rem(dp + k, nd)))
     band[...] = jnp.zeros_like(band)
     slopes[...] = jnp.zeros_like(slopes)
     terms[...] = jnp.zeros_like(terms)

time: 51.9 us -> 52 us (level)
  no operation moved by 1% of the time
where the time goes in v7:
time: 52 us; the launch traced here: 51.8 us
  Pallas kernels  48.1 us (92%)
  other arithmetic  1.98 us (4%)
  local copies, waits for them, and re-layouts  1.07 us (2%)
  between operations  0.65 us (1%)
    pallas_call x1, Pallas kernels, fused(): pl.pallas_call(functools.partial(fused_kernel, nb, nd, cap, shard, main,...  48.1 us
    reshape x1, other arithmetic, fused(): return (act.astype(bf16).reshape(cotangent.shape), grad)  1.98 us
    unnamed x3, local copies, waits for them, and re-layouts  1.07 us

profile of v7, /device:TPU:25, one launch (start us, length us, event | category | flops | bytes accessed | tf_op | source)
XLA Modules:
  0.0 51.8 jit_solution(17717110437391940415)
XLA Ops:
  0.6 48.1 %fused.1 = (f32[4,16,3072]{2,1,0:T(8,128)}, f32[648,192]{1,0:T(8,128)}) custom-call(bf16[8,16,6144]{2,1,0:T(8,128)(2,1)} %bitcast.6, s32[8,16]{1,0:T(8,128)} %bitcast.9, bf16[192,648]{1,0:T(8,128)(2,1)} %bitcast.8, bf16[4,16,3072]{2,1,0:T(8,128)(2,1)} %bitcast.7), custom_call_target="tpu_custom_call" | custom-call | tf_op jit(solution)/shard_map/fused/pallas_call | solution.py:688
  48.8 0.0 copy-start
  48.8 2.0 %convert_bitcast_fusion = bf16[1,4,16,3072]{3,2,1,0:T(8,128)(2,1)} fusion(f32[4,16,3072]{2,1,0:T(8,128)} %get-tuple-element.4), kind=kLoop, calls=%fused_computation | loop fusion | flops 196608 | bytes 1179648 | tf_op jit(solution)/shard_map/reshape | solution.py:733
  50.8 0.0 copy-done
  50.8 1.1 %copy.6 = f32[648,192]{0,1:T(8,128)} copy(f32[648,192]{1,0:T(8,128)S(1)} %copy-done) | data formatting | bytes 995328
Async XLA Ops:
  48.8 2.0 %copy-start = (f32[648,192]{1,0:T(8,128)S(1)}, f32[648,192]{1,0:T(8,128)}, u32[]{:S(2)}) copy-start(f32[648,192]{1,0:T(8,128)} %get-tuple-element.7) | copy-start | bytes 1492996
